TPU v7x, 128 devices: a whole 4x4x4 slice. The times are simulated.
128 devices in a mesh: dp: 8 (over y, z_hi), expert: 16 (over z_lo, x, core).
Axes of the slice: x: 4, y: 4, z: 4 (z_hi: 2, z_lo: 2; z = z_hi * 2 + z_lo), core: 2. Of those that a mesh axis runs over, the one named last changes fastest.
Arguments:
- grad_next: bfloat16 [16384, 4096], P(('dp', 'expert')), may hold values from -6 to 6
- gate_next: float32 [16384, 8], P(('dp', 'expert')), may hold values from 0.05 to 0.5
- expert_ids_next: int32 [16384, 8], P(('dp', 'expert')), may hold values from 0 to 63, all different within a row; in each aligned block of 128 rows (0 to 127, 128 to 255, ...) at most 18 rows name the same one
- hidden_next: bfloat16 [147456, 768], P(('dp', 'expert')), may hold values from -6 to 6
- slot_grads: bfloat16 [147456, 4096], P(('dp', 'expert')), may hold values from -6 to 6
- gate_prev: float32 [16384, 8], P(('dp', 'expert')), may hold values from 0.05 to 0.5
- expert_ids_prev: int32 [16384, 8], P(('dp', 'expert')), may hold values from 0 to 63, all different within a row; in each aligned block of 128 rows (0 to 127, 128 to 255, ...) at most 18 rows name the same one
Outputs:
- down_grad: float32 [64, 768, 4096], P('expert', None, 'dp')
- input_grad: bfloat16 [16384, 4096], P(('dp', 'expert'))
Inputs may be any that keep to these rules, and one draw needn't show every extreme that they name: `expert_ids_next`: each row names 8 different experts. In each aligned block of 128 rows (the tokens of one device) no expert is named by more than 18 rows, and some block names some expert exactly 18 times. `expert_ids_prev`: each row names 8 different experts. In each aligned block of 128 rows (the tokens of one device) no expert is named by more than 18 rows, and some block names some expert exactly 18 times.
All inputs are finite; a program needn't handle non-finite values.
Results may differ from a plain program's by a relative error of at most 0.014.
Values may be sent and summed in bfloat16 or wider, within the bound.
No kernel may reach another device: no remote copies, remote signals or barrier semaphores. Data moves between devices by JAX's collectives and lax.ppermute only.
A program may use at most 256 MiB of HBM per device.

v0:
```python
import jax
import jax.numpy as jnp
from jax import lax
from jax.sharding import PartitionSpec as P

EXP_DEV = 4


def send_rows(expert_ids, experts, capacity):
    flat = expert_ids.reshape(-1)
    onehot = (flat[:, None] == jnp.arange(experts, dtype=jnp.int32)[None, :]).astype(jnp.int32)
    before = jnp.cumsum(onehot, axis=0) - onehot
    ranks = jnp.sum(before * onehot, axis=1)
    return flat * capacity + ranks


def dispatch_rows(outgoing):
    return lax.all_to_all(outgoing, "expert", split_axis=0, concat_axis=0, tiled=True)


def local(
    grad_next, gate_next, expert_ids_next, hidden_next, slot_grads, gate_prev, expert_ids_prev
):
    shards = lax.axis_size("expert")
    experts = EXP_DEV * shards
    capacity = slot_grads.shape[0] // experts
    tok_rows = expert_ids_next.shape[0]
    choose = expert_ids_next.shape[1]
    width = grad_next.shape[1]
    hidden_width = hidden_next.shape[1]
    target = send_rows(expert_ids_next, experts, capacity)
    owner = (
        jnp.zeros((experts * capacity,), jnp.int32)
        .at[target]
        .set(jnp.arange(tok_rows * choose, dtype=jnp.int32) + 1)
    )
    filled = owner > 0
    pair = jnp.maximum(owner - 1, 0)
    token = pair // choose
    factor = jnp.where(filled, gate_next.reshape(-1)[pair], 0.0)
    outgoing = (jnp.take(grad_next, token, axis=0).astype(jnp.float32) * factor[:, None]).astype(
        jnp.bfloat16
    )
    returned = lax.all_to_all(slot_grads, "expert", split_axis=0, concat_axis=0, tiled=True)
    arrived = dispatch_rows(outgoing)
    hidden_four = hidden_next.reshape(shards, EXP_DEV, capacity, hidden_width)
    arrived_four = arrived.reshape(shards, EXP_DEV, capacity, width)
    part = jnp.einsum(
        "secf,secm->efm", hidden_four, arrived_four, preferred_element_type=jnp.float32
    )
    rounded = lax.optimization_barrier(part.astype(jnp.bfloat16)).astype(jnp.float32)
    down_grad = lax.psum_scatter(
        rounded.astype(jnp.bfloat16), "dp", scatter_dimension=2, tiled=True
    ).astype(jnp.float32)
    source = send_rows(expert_ids_prev, experts, capacity)
    picked = jnp.take(returned, source, axis=0).astype(jnp.float32).reshape(tok_rows, choose, width)
    input_grad = jnp.sum(picked * gate_prev[:, :, None], axis=1).astype(jnp.bfloat16)
    return (down_grad, input_grad)


def solution(mesh):
    placed = (
        P(("dp", "expert"), None),
        P(("dp", "expert"), None),
        P(("dp", "expert"), None),
        P(("dp", "expert"), None),
        P(("dp", "expert"), None),
        P(("dp", "expert"), None),
        P(("dp", "expert"), None),
    )
    return jax.shard_map(
        local,
        mesh=mesh,
        in_specs=placed,
        out_specs=(P("expert", None, "dp"), P(("dp", "expert"), None)),
        check_vma=False,
    )
```

profile of v0, /device:TPU:6, one launch (start us, length us, event | category | flops | bytes accessed | tf_op | source)
XLA Modules:
  0.0 599.3 jit_solution(4971794674968774820)
XLA Ops:
  7.2 0.9 copy.62
  8.2 0.7 broadcast_multiply_fusion.1
  9.0 18.0 %reduce-window.14 = s32[64,8,128]{2,1,0:T(8,128)S(1)} reduce-window(s32[64,8,128]{2,1,0:T(8,128)S(1)} %fusion.8, s32[]{:T(128)} %constant.54.clone.1), window={size=1x1x128 pad=0_0x0_0x127_0}, to_apply=%region_0.0 | reduce-window | flops 8323072 | bytes 524292 | tf_op jit(solution)/shard_map/reduce-window
  27.1 0.1 copy.64
  27.8 4.3 scatter_custom_fusion
  32.2 0.8 copy.66
  33.1 4.6 gather_fusion.1
  37.9 8.0 %gather_fusion = bf16[1152,4096]{1,0:T(8,128)(2,1)} fusion(bf16[128,4096]{1,0:T(8,128)(2,1)S(1)} %copy-done, s32[2048]{0:T(1024)S(1)} %pad_clamp_fusion.1), kind=kCustom, calls=%fused_computation | custom fusion | bytes 18878976 | tf_op jit(solution)/shard_map/jit(_take)/gather | solution.py:41
  45.9 13.9 %multiply_convert_fusion = bf16[16,72,4096]{2,1,0:T(8,128)(2,1)} fusion(f32[16,72]{1,0:T(8,128)S(1)} %mul.57, bf16[16,72,4096]{2,1,0:T(8,128)(2,1)} %bitcast.56, pred[16,72]{1,0:T(8,128)(4,1)S(1)} %broadcast_in_dim.36), kind=kLoop, calls=%fused_computation.6 | loop fusion | flops 18874368 | bytes 18880128 | tf_op jit(solution)/shard_map/convert_element_type | solution.py:41
  59.8 6.1 %all-to-all-start = ((bf16[16,72,4096]{2,1,0:T(8,128)(2,1)}), bf16[16,72,4096]{2,1,0:T(8,128)(2,1)}, u32[]{:S(2)}, u32[]{:S(2)}) async-start(bf16[16,72,4096]{2,1,0:T(8,128)(2,1)} %multiply_convert_fusion), calls=%async_computation | async-start | bytes 18874368 | tf_op jit(solution)/shard_map/all_to_all | solution.py:18
  66.0 0.2 reduce-scatter.2.cloned.1.call-start
  66.2 2.5 reshape.147
  68.7 121.3 %all-to-all-done = bf16[16,72,4096]{2,1,0:T(8,128)(2,1)} async-done(((bf16[16,72,4096]{2,1,0:T(8,128)(2,1)}), bf16[16,72,4096]{2,1,0:T(8,128)(2,1)}, u32[]{:S(2)}, u32[]{:S(2)}) %all-to-all-start) | async-done | bytes 9437216 | tf_op jit(solution)/shard_map/all_to_all | solution.py:18
  190.0 12.4 %copy.67 = bf16[16,72,4096]{2,0,1:T(8,128)(2,1)} copy(bf16[16,72,4096]{2,1,0:T(8,128)(2,1)} %all-to-all-done) | data formatting | bytes 18874368 | tf_op jit(solution)/shard_map/all_to_all | solution.py:18
  202.4 22.2 %fusion = bf16[4,768,4096]{1,2,0:T(8,128)(2,1)} fusion(bf16[16,4,18,4096]{3,0,2,1:T(8,128)(2,1)} %bitcast.58, bf16[16,4,18,768]{3,2,1,0:T(8,128)(2,1)S(1)} %reshape.147), kind=kOutput, calls=%fused_computation.5 | convolution fusion | flops 7260340224 | bytes 36372480 | tf_op jit(solution)/shard_map/secf,secm->efm/dot_general | solution.py:48
  224.7 7.6 %all-to-all-start.1 = ((bf16[16,72,4096]{2,1,0:T(8,128)(2,1)}), bf16[16,72,4096]{2,1,0:T(8,128)(2,1)}, u32[]{:S(2)}, u32[]{:S(2)}) async-start(bf16[16,72,4096]{2,1,0:T(8,128)(2,1)} %bitcast.57), calls=%async_computation.2 | async-start | bytes 18874368 | tf_op jit(solution)/shard_map/all_to_all | solution.py:44
  232.6 18.0 %reduce-window.16 = s32[64,8,128]{2,1,0:T(8,128)S(1)} reduce-window(s32[64,8,128]{2,1,0:T(8,128)S(1)} %fusion.9, s32[]{:T(128)} %constant.54.clone.1), window={size=1x1x128 pad=0_0x0_0x127_0}, to_apply=%region_5.6 | reduce-window | flops 8323072 | bytes 524292 | tf_op jit(solution)/shard_map/reduce-window.2
  250.8 0.1 copy.71
  251.6 0.1 copy.74
  251.9 104.3 %all-to-all-done.1 = bf16[16,72,4096]{2,1,0:T(8,128)(2,1)} async-done(((bf16[16,72,4096]{2,1,0:T(8,128)(2,1)}), bf16[16,72,4096]{2,1,0:T(8,128)(2,1)}, u32[]{:S(2)}, u32[]{:S(2)}) %all-to-all-start.1) | async-done | bytes 9437216 | tf_op jit(solution)/shard_map/all_to_all | solution.py:44
  356.2 20.1 %gather_fusion.2 = bf16[1024,4096]{1,0:T(8,128)(2,1)} fusion(bf16[1152,4096]{1,0:T(8,128)(2,1)} %bitcast.12, s32[1024]{0:T(1024)S(1)} %broadcast_clamp_fusion), kind=kCustom, calls=%fused_computation.2 | custom fusion | bytes 16781312 | tf_op jit(solution)/shard_map/jit(_take)/gather | solution.py:56
  376.3 15.4 %multiply_reduce_fusion = bf16[128,4096]{1,0:T(8,128)(2,1)} fusion(bf16[1024,4096]{1,0:T(8,128)(2,1)} %gather_fusion.2, f32[128,8]{1,0:T(8,128)S(1)} %copy.76, pred[128,8]{1,0:T(8,128)(4,1)S(1)} %copy.74), kind=kLoop, calls=%fused_computation.7 | loop fusion | flops 16252928 | bytes 9442304 | tf_op jit(solution)/shard_map/reduce_sum | solution.py:57
  391.7 195.4 %reduce-scatter.2.cloned.1.call-done = bf16[4,768,512]{1,2,0:T(8,128)(2,1)} async-done(((bf16[4,768,4096]{1,2,0:T(8,128)(2,1)}), bf16[4,768,512]{1,2,0:T(8,128)(2,1)}) %reduce-scatter.2.cloned.1.call-update) | async-done | bytes 3145744 | tf_op jit(solution)/shard_map/reduce_scatter | solution.py:52
  587.1 5.4 copy.77
  (49 shorter events, 2.4 us)
Async XLA Ops:
  7.2 30.7 %copy-start = (bf16[128,4096]{1,0:T(8,128)(2,1)S(1)}, bf16[128,4096]{1,0:T(8,128)(2,1)}, u32[]{:S(2)}) copy-start(bf16[128,4096]{1,0:T(8,128)(2,1)} %param.7) | copy-start | bytes 3145732
  59.8 130.2 %all-to-all-start = ((bf16[16,72,4096]{2,1,0:T(8,128)(2,1)}), bf16[16,72,4096]{2,1,0:T(8,128)(2,1)}, u32[]{:S(2)}, u32[]{:S(2)}) async-start(bf16[16,72,4096]{2,1,0:T(8,128)(2,1)} %multiply_convert_fusion), calls=%async_computation | async-start | bytes 18874368 | tf_op jit(solution)/shard_map/all_to_all | solution.py:18
  66.0 521.1 %reduce-scatter.2.cloned.1.call-start = ((), (), s32[]{:S(2)}) async-start(), calls=%async_computation.3 | async-start | bytes 28311552 | tf_op jit(solution)/shard_map/reduce_scatter | solution.py:52
  224.6 7.7 %copy-start.2 = (s32[128,8]{0,1:T(8,128)S(1)}, s32[128,8]{0,1:T(8,128)}, u32[]{:S(2)}) copy-start(s32[128,8]{0,1:T(8,128)} %param.13) | copy-start | bytes 12292
  224.7 27.1 %copy-start.3 = (f32[128,8]{0,1:T(8,128)S(1)}, f32[128,8]{0,1:T(8,128)}, u32[]{:S(2)}) copy-start(f32[128,8]{0,1:T(8,128)} %param.12) | copy-start | bytes 12292
  224.7 131.5 %all-to-all-start.1 = ((bf16[16,72,4096]{2,1,0:T(8,128)(2,1)}), bf16[16,72,4096]{2,1,0:T(8,128)(2,1)}, u32[]{:S(2)}, u32[]{:S(2)}) async-start(bf16[16,72,4096]{2,1,0:T(8,128)(2,1)} %bitcast.57), calls=%async_computation.2 | async-start | bytes 18874368 | tf_op jit(solution)/shard_map/all_to_all | solution.py:44
  356.2 236.3 %copy-start.1 = (bf16[128,4096]{1,0:T(8,128)(2,1)S(1)}, bf16[128,4096]{1,0:T(8,128)(2,1)}, u32[]{:S(2)}) copy-start(bf16[128,4096]{1,0:T(8,128)(2,1)} %param.7) | copy-start | bytes 3145732
Sparse Core Ops, SparseCore 0:
  224.8 362.2 reduce-scatter.1
where the time goes:
time: 600 us; the launch traced here: 599 us
  waiting for transfers between devices  421 us (70%)
  other arithmetic  66.6 us (11%)
  local copies, waits for them, and re-layouts  61.2 us (10%)
  matrix products  22.2 us (4%)
  between operations  14.3 us (2%)
  starting transfers between devices  14 us (2%)
    reduce_scatter x1, waiting for transfers between devices, local(): lax.psum_scatter(rounded.astype(jnp.bfloat16), 'dp', scatter_dimension=2,...  195 us
    all_to_all x1, waiting for transfers between devices, dispatch_rows(): lax.all_to_all(outgoing, 'expert', split_axis=0, concat_axis=0, tiled=True)  121 us
    all_to_all x1, waiting for transfers between devices, local(): lax.all_to_all(slot_grads, 'expert', split_axis=0, concat_axis=0, tiled=T...  104 us
    another operation x6, other arithmetic  36.3 us
    dot_general x1, matrix products, local(): jnp.einsum('secf,secm->efm', hidden_four, arrived_four, preferred_element...  22.2 us
    gather x1, local copies, waits for them, and re-layouts, local(): jnp.take(returned, source, axis=0).astype(jnp.float32)  20.1 us
    reduce_sum x1, other arithmetic, local(): jnp.sum(picked * gate_prev[:, :, None], axis=1).astype(jnp.bfloat16)  15.4 us
    convert_element_type x1, other arithmetic, local(): (jnp.take(grad_next, token, axis=0).astype(jnp.float32) * factor[:, None]...  13.9 us
  transfers between devices with their start and end apart: 3, of which 3 were waited for; matrix products, arithmetic and copies ran while one was open for 10% of the time, Pallas kernels for 0%

commit v1 on v0

v1 whole, which is shorter than its diff:
```python
import functools

import jax
import jax.numpy as jnp
from jax import lax
from jax.experimental import pallas as pl
from jax.experimental.pallas import tpu as pltpu
from jax.sharding import PartitionSpec as P

E = 4
CAP = 18
SLOT = E * CAP
PAIR = 2 * SLOT
TOK = 128
TOP = 8
D = 4096
HALF = D // 2
COLS = 512
FFW = 768
NDP = 8
NEX = 16
X = 4
ROWS = NEX * CAP
SIB = ROWS // 2
LONG = TOK + 16
QUAD = 4
BATCH = 4

VMEM = 56 * 1024 * 1024


def ex_perm(dzl, dx, dc):
    pairs = []
    for zl in range(2):
        for x in range(X):
            for c in range(2):
                src = ((zl ^ dzl) * X + (x + dx) % X) * 2 + (c ^ dc)
                pairs.append((src, (zl * X + x) * 2 + c))
    return pairs


def dp_perm(dy, dzh):
    pairs = []
    for y in range(4):
        for zh in range(2):
            pairs.append((((y + dy) % 4) * 2 + (zh ^ dzh), y * 2 + zh))
    return pairs


def ex_from(value, dzl, dx, dc):
    return lax.ppermute(value, "expert", ex_perm(dzl, dx, dc))


def dp_from(value, dy, dzh):
    return lax.ppermute(value, "dp", dp_perm(dy, dzh))


def slot_weights(lines, first_expert):
    slot = lax.broadcasted_iota(jnp.int32, (SLOT, TOK), 0)
    expert = (
        (slot >= CAP).astype(jnp.int32)
        + (slot >= 2 * CAP).astype(jnp.int32)
        + (slot >= 3 * CAP).astype(jnp.int32)
    )
    place = (slot - CAP * expert).astype(jnp.float32)
    name = (expert + first_expert).astype(jnp.float32)
    gate = jnp.zeros((SLOT, TOK), jnp.float32)
    named = jnp.zeros((SLOT, TOK), jnp.float32)
    for k in range(TOP):
        same = lines[k] == name
        named = jnp.where(same, 1.0, named)
        gate = jnp.where(same, lines[TOP + k], gate)
    earlier = (
        lax.broadcasted_iota(jnp.int32, (TOK, TOK), 0)
        < lax.broadcasted_iota(jnp.int32, (TOK, TOK), 1)
    ).astype(jnp.bfloat16)
    rank = jnp.dot(named.astype(jnp.bfloat16), earlier, preferred_element_type=jnp.float32)
    return jnp.where(rank == place, gate, 0.0)


def cut_columns_kernel(targets, grad_ref, meta_ref, *out_refs):
    table = meta_ref[2 * TOP :, :].astype(jnp.bfloat16)
    table = jnp.concatenate([table, jnp.zeros((2 * TOP, COLS - TOK), jnp.bfloat16)], axis=1)
    outs = [ref.at[dy] for ref in out_refs for dy in range(4)]
    for i, out in enumerate(outs):
        at = pl.multiple_of(targets[i] * COLS, COLS)
        out[:TOK, :] = grad_ref[:, pl.ds(at, COLS)]
        out[TOK:, :] = table


def cut_columns(targets, grad, meta):
    shapes = [(4, LONG, COLS)] * 2
    return pl.pallas_call(
        cut_columns_kernel,
        grid_spec=pltpu.PrefetchScalarGridSpec(
            num_scalar_prefetch=1,
            grid=(1,),
            in_specs=[
                pl.BlockSpec((TOK, D), lambda i, s: (0, 0)),
                pl.BlockSpec((4 * TOP, TOK), lambda i, s: (0, 0)),
            ],
            out_specs=[pl.BlockSpec(s, lambda i, _, n=len(s): (0,) * n) for s in shapes],
        ),
        out_shape=[jax.ShapeDtypeStruct(s, jnp.bfloat16) for s in shapes],
        compiler_params=pltpu.CompilerParams(vmem_limit_bytes=VMEM),
    )(targets, grad, meta)


def return_route_kernel(scalars, meta_ref, out_ref):
    core = scalars[0]
    for i in range(8):
        lines = [meta_ref[i, k : k + 1, :] for k in range(2 * TOP)]
        for j in range(2):
            gate = slot_weights(lines, scalars[1 + j])
            none = jnp.zeros_like(gate)
            both = jnp.concatenate(
                [jnp.where(core == 0, gate, none), jnp.where(core == 1, gate, none)], axis=0
            )
            out_ref[i, j] = both.astype(jnp.bfloat16)


def return_route(scalars, meta):
    return pl.pallas_call(
        return_route_kernel,
        grid_spec=pltpu.PrefetchScalarGridSpec(
            num_scalar_prefetch=1,
            grid=(1,),
            in_specs=[pl.BlockSpec((8, 2 * TOP, TOK), lambda i, s: (0, 0, 0))],
            out_specs=pl.BlockSpec((8, 2, PAIR, TOK), lambda i, s: (0, 0, 0, 0)),
        ),
        out_shape=jax.ShapeDtypeStruct((8, 2, PAIR, TOK), jnp.bfloat16),
        compiler_params=pltpu.CompilerParams(vmem_limit_bytes=VMEM),
    )(scalars, meta)


def combine_kernel(scalars, weight_ref, own_ref, sib_ref, *out_refs, outs):
    chunk = 1024
    for at in range(0, D, chunk):
        total = jnp.zeros((TOK, chunk), jnp.float32)
        for j, rows in enumerate((own_ref, sib_ref)):
            total += lax.dot_general(
                weight_ref[0, j],
                rows[:, at : at + chunk],
                (((0,), (0,)), ((), ())),
                preferred_element_type=jnp.float32,
            )
        for (low, high), ref in zip(outs, out_refs):
            if low <= at < high:
                ref[0, :, at - low : at - low + chunk] = total.astype(jnp.bfloat16)


def combine(pairs, weights, own, sib, first, steps, outs):
    out_specs = [pl.BlockSpec((1, TOK, high - low), lambda i, s: (i, 0, 0)) for low, high in outs]
    return pl.pallas_call(
        functools.partial(combine_kernel, outs=outs),
        grid_spec=pltpu.PrefetchScalarGridSpec(
            num_scalar_prefetch=1,
            grid=(steps,),
            in_specs=[
                pl.BlockSpec((1, 2, PAIR, TOK), lambda i, s: (first + i, 0, 0, 0)),
                pl.BlockSpec((PAIR, D), lambda i, s: (s[first + i], 0)),
                pl.BlockSpec((PAIR, D), lambda i, s: (s[first + i], 0)),
            ],
            out_specs=out_specs,
        ),
        out_shape=[
            jax.ShapeDtypeStruct((steps, TOK, high - low), jnp.bfloat16) for low, high in outs
        ],
        compiler_params=pltpu.CompilerParams(vmem_limit_bytes=VMEM),
    )(pairs, weights, own, sib)


def sent_kernel(scalars, spread_ref, *refs):
    tok_refs, out_ref = refs[:8], refs[8]
    quads = []
    for quad in range(2):
        route = []
        for i in range(QUAD):
            table = tok_refs[quad * QUAD + i][0, TOK:, :TOK].astype(jnp.float32)
            lines = [table[k : k + 1, :] for k in range(2 * TOP)]
            gate = slot_weights(lines, scalars[0]).astype(jnp.bfloat16)
            rows = jnp.dot(spread_ref[i], gate, preferred_element_type=jnp.float32)
            route.append(rows.astype(jnp.bfloat16))
        tokens = jnp.concatenate(
            [tok_refs[quad * QUAD + i][0, :TOK, :] for i in range(QUAD)], axis=0
        )
        quads.append(
            jnp.dot(
                jnp.concatenate(route, axis=1), tokens, preferred_element_type=jnp.float32
            )
        )
    for e in range(E):
        rows = [quad[e * SLOT : (e + 1) * SLOT, :] for quad in quads]
        out_ref[0, e] = jnp.concatenate(rows, axis=0).astype(jnp.bfloat16)


def build_sent(scalars, spread, tokens):
    return pl.pallas_call(
        sent_kernel,
        grid_spec=pltpu.PrefetchScalarGridSpec(
            num_scalar_prefetch=1,
            grid=(NDP,),
            in_specs=[pl.BlockSpec((QUAD, QUAD * SLOT, SLOT), lambda g, s: (0, 0, 0))]
            + [pl.BlockSpec((1, LONG, COLS), lambda g, s: (g, 0, 0)) for _ in range(8)],
            out_specs=pl.BlockSpec((1, E, SIB, COLS), lambda g, s: (g, 0, 0, 0)),
        ),
        out_shape=jax.ShapeDtypeStruct((NDP, E, SIB, COLS), jnp.bfloat16),
        compiler_params=pltpu.CompilerParams(vmem_limit_bytes=VMEM),
    )(scalars, spread, *tokens)


def weight_kernel(near_ref, far_ref, zero_ref, one_ref, low_ref, high_ref, three_ref, *refs):
    out_ref = refs[-1]
    two = jnp.where(pl.program_id(0) < E // 2, low_ref[0], high_ref[0])
    hidden = jnp.concatenate([zero_ref[0], one_ref[0], two, three_ref[0]], axis=0)
    sent = jnp.concatenate(
        [ref[g, 0] for g in range(BATCH) for ref in (near_ref, far_ref)], axis=0
    )
    total = lax.dot_general(
        hidden, sent, (((0,), (0,)), ((), ())), preferred_element_type=jnp.float32
    )
    if len(refs) > 1:
        total += refs[0][0]
    out_ref[0] = total


def weight_grad(sents, batch, hiddens, before):
    result = pl.BlockSpec((1, FFW, COLS), lambda e: (e, 0, 0))
    rows = pl.BlockSpec((1, ROWS, FFW), lambda e: (e, 0, 0))
    return pl.pallas_call(
        weight_kernel,
        grid=(E,),
        in_specs=[
            pl.BlockSpec((BATCH, 1, SIB, COLS), lambda e: (batch, e, 0, 0)),
            pl.BlockSpec((BATCH, 1, SIB, COLS), lambda e: (batch, e, 0, 0)),
            rows,
            rows,
            pl.BlockSpec((1, ROWS, FFW), lambda e: (jnp.minimum(e, E // 2 - 1), 0, 0)),
            pl.BlockSpec((1, ROWS, FFW), lambda e: (jnp.maximum(e - E // 2, 0), 0, 0)),
            rows,
        ]
        + [result] * len(before),
        out_specs=result,
        out_shape=jax.ShapeDtypeStruct((E, FFW, COLS), jnp.float32),
        compiler_params=pltpu.CompilerParams(vmem_limit_bytes=VMEM),
    )(*sents, *hiddens, *before)


def local(
    grad_next, gate_next, expert_ids_next, hidden_next, slot_grads, gate_prev, expert_ids_prev
):
    me = lax.axis_index("expert")
    zl, x, c = me // (2 * X), (me // 2) % X, me % 2
    dp = lax.axis_index("dp")
    y, zh = dp // 2, dp % 2
    first = (me * E).astype(jnp.int32)

    meta = jnp.concatenate(
        [
            expert_ids_prev.astype(jnp.float32),
            gate_prev,
            expert_ids_next.astype(jnp.float32),
            gate_next,
        ],
        axis=1,
    ).T

    targets = [((y - dy) % 4) * 2 + z for z in (zh, 1 - zh) for dy in range(4)]
    same, other = cut_columns(jnp.stack(targets).astype(jnp.int32), grad_next, meta)
    other = dp_from(other, 0, 1)
    meta = meta[: 2 * TOP]
    meta = jnp.stack([meta, ex_from(meta, 1, 0, 0)])
    meta = jnp.stack([meta] + [ex_from(meta, 0, dx, 0) for dx in (1, 2, 3)])
    meta_prev = meta.reshape(8, 2 * TOP, TOK)

    sibling = ex_from(slot_grads, 0, 0, 1)
    weights = return_route(
        jnp.stack([c, first, (me ^ 1) * E]).astype(jnp.int32), meta_prev
    )
    pairs = jnp.stack(
        [(zl ^ dzl) * X + (x + dx) % X for dx in range(X) for dzl in range(2)]
    ).astype(jnp.int32)
    halves = [(0, HALF), (HALF, D)]

    def part(dx):
        return combine(pairs, weights, slot_grads, sibling, 2 * dx, 2, halves)

    def add(*values):
        return sum(v.astype(jnp.float32) for v in values).astype(jnp.bfloat16)

    def after(value, *earlier):
        return lax.optimization_barrier((value, earlier))[0]

    left, right = part(2)
    both = after(jnp.stack([same, other], axis=1), left, right)
    own = [both[0]] + [dp_from(both[dy], dy, 0) for dy in (1, 2, 3)]
    own = jnp.stack(own, axis=1).reshape(NDP, LONG, COLS)
    left, right = ex_from(left, 0, 3, 0), ex_from(right, 0, 1, 0)
    up, down, here = part(1), part(3), part(0)

    blocks = jnp.stack(
        [
            ((zl ^ dzl) * X + (x + dx) % X) * 2 + (c ^ dc)
            for dzl in range(2)
            for dc in range(2)
            for dx in range(X)
        ]
    ).reshape(1, NEX, 1)
    source = (
        blocks * SLOT
        + jnp.arange(E, dtype=jnp.int32)[:, None, None] * CAP
        + jnp.arange(CAP, dtype=jnp.int32)[None, None, :]
    ).reshape(-1)
    move = (source[:, None] == jnp.arange(NEX * SLOT, dtype=jnp.int32)[None, :]).astype(
        jnp.bfloat16
    )
    mine = jnp.dot(move, hidden_next, preferred_element_type=jnp.float32).astype(jnp.bfloat16)
    mine = after(mine.reshape(E, ROWS, FFW), own)

    def to_sides(zero):
        return dp_from(zero, 1, 0), dp_from(zero, 3, 0)

    def onward(one, three):
        return dp_from(one[: E // 2], 1, 0), dp_from(three[E // 2 :], 3, 0)

    one, three = to_sides(mine)
    low, high = onward(one, three)

    over = ex_from(own, 1, 0, 0)
    across = dp_from(after(mine, over), 0, 1)
    own = after(own, left, right)
    near = [own, ex_from(own, 0, 1, 0), None, ex_from(own, 0, 3, 0)]
    near[2] = jnp.concatenate(
        [ex_from(near[1][:BATCH], 0, 1, 0), ex_from(near[3][BATCH:], 0, 3, 0)]
    )
    over_late = after(over, near[2], one, three)
    far = [
        over,
        ex_from(over_late, 0, 1, 0),
        ex_from(after(near[2], across), 1, 0, 0),
        ex_from(over_late, 0, 3, 0),
    ]
    near = near[:1] + near[1:] + [ex_from(t, 0, 0, 1) for t in near]
    far_all = far + [ex_from(t, 0, 0, 1) for t in far]

    across = after(across, low, high)
    across_one, across_three = to_sides(across)
    across_low, across_high = onward(across_one, across_three)

    up = [add(up[0], left), up[1]]
    down = [down[0], add(down[1], right)]
    row = jnp.arange(QUAD * SLOT, dtype=jnp.int32)[None, :, None]
    slot = jnp.arange(SLOT, dtype=jnp.int32)[None, None, :]
    block = jnp.arange(QUAD, dtype=jnp.int32)[:, None, None]
    spread = (
        (row % SLOT // CAP == block) & (row // SLOT * CAP + row % CAP == slot)
    ).astype(jnp.bfloat16)
    crossed, sents = [], []
    gates = [(far[1], far[3], across, low, high, *near), (far[2], *far_all)]
    for i in range(2):
        u = ex_from(after(up[i], *gates[i], *sents), 0, 3, 0)
        d = ex_from(after(down[i], *gates[i], *sents), 0, 1, 0)
        sents.append(build_sent(first[None], spread, (near, far_all)[i]))
        side = add(here[i][1], u[1], d[1])
        if i:
            side = after(side, *sents)
        side = ex_from(side, 1, 0, 0)
        crossed.append(add(here[i][0], u[0], d[0], side))
    input_grad = jnp.concatenate(crossed, axis=1)
    down_grad = weight_grad(sents, 0, (mine, one, low, high, three), [])
    down_grad = weight_grad(
        sents, 1, (across, across_one, across_low, across_high, across_three), [down_grad]
    )
    return down_grad, input_grad


def solution(mesh):
    rows = P(("dp", "expert"), None)
    return jax.shard_map(
        local,
        mesh=mesh,
        in_specs=(rows,) * 7,
        out_specs=(P("expert", None, "dp"), rows),
        check_vma=False,
    )
```

time: 600 us -> 247 us (0.41)
  waiting for transfers between devices: 421 us -> 103 us
  Pallas kernels: 0 us -> 72 us
  local copies, waits for them, and re-layouts: 61.2 us -> 7.55 us
  other arithmetic: 66.6 us -> 18.7 us
  starting transfers between devices: 14 us -> 40.7 us
  matrix products: 22.2 us -> 2.6 us
  between operations: 14.3 us -> 1.11 us
    all_to_all x2 -> x0, waiting for transfers between devices: 226 us -> none  [the longest x1 121 us: dispatch_rows(): lax.all_to_all(outgoing, 'expert', split_axis=0, concat_axis=0, tiled=True)]
    reduce_scatter x1 -> x0, waiting for transfers between devices: 195 us -> none  [local(): lax.psum_scatter(rounded.astype(jnp.bfloat16), 'dp', scatter_dimension=2,...]
    ppermute x0 -> x42, waiting for transfers between devices: none -> 103 us  [the longest x29 62.1 us: ex_from(): return lax.ppermute(value, 'expert', ex_perm(dzl, dx, dc))]
    pallas_call x0 -> x10, Pallas kernels: none -> 72 us  [the longest x2 26.9 us: build_sent(): pl.pallas_call(sent_kernel, grid_spec=pltpu.PrefetchScalarGridSpec(num_sc...]
    ppermute x0 -> x42, starting transfers between devices: none -> 40.7 us  [the longest x29 20.3 us: ex_from(): return lax.ppermute(value, 'expert', ex_perm(dzl, dx, dc))]
    another operation x6 -> x5, other arithmetic: 36.3 us -> 2.68 us  [the longest x1 1.29 us: local(): own = jnp.stack(own, axis=1).reshape(NDP, LONG, COLS)]
    gather x3 -> x0, local copies, waits for them, and re-layouts: 32.7 us -> none  [the longest x1 20.1 us: local(): jnp.take(returned, source, axis=0).astype(jnp.float32)]
    dot_general x1, matrix products: 22.2 us -> 2.6 us  [local(): jnp.dot(move, hidden_next, preferred_element_type=jnp.float32)]
  transfers between devices with their start and end apart: 3 -> 42, of which waited for: 3 -> 19; matrix products, arithmetic and copies ran while one was open for 10% -> 9% of each run, Pallas kernels for 0% -> 27%
where the time goes in v1:
time: 247 us; the launch traced here: 246 us
  waiting for transfers between devices  103 us (42%)
  Pallas kernels  72 us (29%)
  starting transfers between devices  40.7 us (16%)
  other arithmetic  18.7 us (8%)
  local copies, waits for them, and re-layouts  7.55 us (3%)
  matrix products  2.6 us (1%)
    ppermute x29, waiting for transfers between devices, ex_from(): return lax.ppermute(value, 'expert', ex_perm(dzl, dx, dc))  62.1 us
    ppermute x13, waiting for transfers between devices, dp_from(): return lax.ppermute(value, 'dp', dp_perm(dy, dzh))  41.3 us
    pallas_call x2, Pallas kernels, build_sent(): pl.pallas_call(sent_kernel, grid_spec=pltpu.PrefetchScalarGridSpec(num_sc...  26.9 us
    ppermute x29, starting transfers between devices, ex_from(): return lax.ppermute(value, 'expert', ex_perm(dzl, dx, dc))  20.3 us
    ppermute x13, starting transfers between devices, dp_from(): return lax.ppermute(value, 'dp', dp_perm(dy, dzh))  20.3 us
    pallas_call x2, Pallas kernels, weight_grad(): pl.pallas_call(weight_kernel, grid=(E,), in_specs=[pl.BlockSpec((BATCH, 1...  20.3 us
    pallas_call x4, Pallas kernels, combine(): pl.pallas_call(functools.partial(combine_kernel, outs=outs), grid_spec=pl...  18.9 us
    convert_element_type x6, other arithmetic, add(): return sum((v.astype(jnp.float32) for v in values)).astype(jnp.bfloat16)  11.5 us
  transfers between devices with their start and end apart: 42, of which 19 were waited for; matrix products, arithmetic and copies ran while one was open for 9% of the time, Pallas kernels for 27%

profile of v1, /device:TPU:6, one launch (start us, length us, event | category | flops | bytes accessed | tf_op | source)
XLA Modules:
  0.0 246.0 jit_solution(11134150911872152631)
XLA Ops:
  8.6 3.6 %collective-permute-start = (bf16[4,144,512]{2,1,0:T(8,128)(2,1)}, bf16[4,144,512]{2,1,0:T(8,128)(2,1)S(1)}, u32[]{:S(2)}, u32[]{:S(2)}) collective-permute-start(bf16[4,144,512]{2,1,0:T(8,128)(2,1)} %get-tuple-element.25), channel_id=1, source_target_pairs={{16,0},{0,16},{48,32},{32,48},{80,64},{64,80},{112,96},{96,112},{1... | collective-permute-start | bytes 1769480 | tf_op jit(solution)/shard_map/ppermute | solution.py:55
  22.0 3.9 %collective-permute-done = bf16[4,144,512]{2,1,0:T(8,128)(2,1)S(1)} collective-permute-done((bf16[4,144,512]{2,1,0:T(8,128)(2,1)}, bf16[4,144,512]{2,1,0:T(8,128)(2,1)S(1)}, u32[]{:S(2)}, u32[]{:S(2)}) %collective-permute-start) | collective-permute-done | bytes 589856 | tf_op jit(solution)/shard_map/ppermute | solution.py:55
  26.0 4.7 %shard_map.88 = (bf16[2,128,2048]{2,1,0:T(8,128)(2,1)}, bf16[2,128,2048]{2,1,0:T(8,128)(2,1)}) custom-call(s32[8]{0:T(128)} %stack.180.scalars, bf16[8,2,144,128]{3,2,1,0:T(8,128)(2,1)} %shard_map.87.weight_ref, bf16[1152,4096]{1,0:T(8,128)(2,1)} %own_ref.7, bf16[1152,4096]{1,0:T(8,128)(2,1)} %collective-permute-done.5.sib_ref), custom_call_target="tpu_custom_call" | custom-call | tf_op jit(solution)/shard_map/pallas_call | solution.py:154
  40.5 7.5 %collective-permute-done.6 = bf16[2,144,512]{2,1,0:T(8,128)(2,1)} collective-permute-done((bf16[2,144,512]{2,1,0:T(8,128)(2,1)}, bf16[2,144,512]{2,1,0:T(8,128)(2,1)}, u32[]{:S(2)}, u32[]{:S(2)}) %collective-permute-start.6) | collective-permute-done | bytes 294944 | tf_op jit(solution)/shard_map/ppermute | solution.py:55
  48.0 3.7 %collective-permute-done.8 = bf16[2,144,512]{2,1,0:T(8,128)(2,1)} collective-permute-done((bf16[2,144,512]{2,1,0:T(8,128)(2,1)}, bf16[2,144,512]{2,1,0:T(8,128)(2,1)}, u32[]{:S(2)}, u32[]{:S(2)}) %collective-permute-start.8) | collective-permute-done | bytes 294944 | tf_op jit(solution)/shard_map/ppermute | solution.py:55
  58.0 4.3 %collective-permute-done.10 = bf16[2,128,2048]{2,1,0:T(8,128)(2,1)S(1)} collective-permute-done((bf16[2,128,2048]{2,1,0:T(8,128)(2,1)}, bf16[2,128,2048]{2,1,0:T(8,128)(2,1)S(1)}, u32[]{:S(2)}, u32[]{:S(2)}) %collective-permute-start.10) | collective-permute-done | bytes 1048608 | tf_op jit(solution)/shard_map/ppermute | solution.py:51
  66.5 14.6 %collective-permute-done.19.refs_0_ = bf16[8,144,512]{2,1,0:T(8,128)(2,1)S(1)} collective-permute-done((bf16[8,144,512]{2,1,0:T(8,128)(2,1)S(1)}, bf16[8,144,512]{2,1,0:T(8,128)(2,1)S(1)}, u32[]{:S(2)}, u32[]{:S(2)}) %collective-permute-start.19) | collective-permute-done | bytes 1179680 | tf_op jit(solution)/shard_map/ppermute | solution.py:51
  84.0 6.1 %collective-permute-done.11.refs_1_ = bf16[8,144,512]{2,1,0:T(8,128)(2,1)S(1)} collective-permute-done((bf16[8,144,512]{2,1,0:T(8,128)(2,1)S(1)}, bf16[8,144,512]{2,1,0:T(8,128)(2,1)S(1)}, u32[]{:S(2)}, u32[]{:S(2)}) %collective-permute-start.11) | collective-permute-done | bytes 1179680 | tf_op jit(solution)/shard_map/ppermute | solution.py:51
  90.3 6.1 %collective-permute-done.20.one_ref = bf16[4,288,768]{2,1,0:T(8,128)(2,1)S(1)} collective-permute-done((bf16[4,288,768]{2,1,0:T(8,128)(2,1)S(1)}, bf16[4,288,768]{2,1,0:T(8,128)(2,1)S(1)}, u32[]{:S(2)}, u32[]{:S(2)}) %collective-permute-start.20) | collective-permute-done | bytes 1769504 | tf_op jit(solution)/shard_map/ppermute | solution.py:55
  98.6 8.6 %collective-permute-done.12 = bf16[4,144,512]{2,1,0:T(8,128)(2,1)S(1)} collective-permute-done((bf16[4,144,512]{2,1,0:T(8,128)(2,1)S(1)}, bf16[4,144,512]{2,1,0:T(8,128)(2,1)S(1)}, u32[]{:S(2)}, u32[]{:S(2)}) %collective-permute-start.12) | collective-permute-done | bytes 589856 | tf_op jit(solution)/shard_map/ppermute | solution.py:51
  111.6 6.3 %collective-permute-done.30.low_ref = bf16[2,288,768]{2,1,0:T(8,128)(2,1)S(1)} collective-permute-done((bf16[2,288,768]{2,1,0:T(8,128)(2,1)S(1)}, bf16[2,288,768]{2,1,0:T(8,128)(2,1)S(1)}, u32[]{:S(2)}, u32[]{:S(2)}) %collective-permute-start.30) | collective-permute-done | bytes 884768 | tf_op jit(solution)/shard_map/ppermute | solution.py:55
  119.0 3.2 %collective-permute-done.23.zero_ref = bf16[4,288,768]{2,1,0:T(8,128)(2,1)S(1)} collective-permute-done((bf16[4,288,768]{2,1,0:T(8,128)(2,1)S(1)}, bf16[4,288,768]{2,1,0:T(8,128)(2,1)S(1)}, u32[]{:S(2)}, u32[]{:S(2)}) %collective-permute-start.23) | collective-permute-done | bytes 1769504 | tf_op jit(solution)/shard_map/ppermute | solution.py:55
  122.8 7.0 %collective-permute-done.31.high_ref = bf16[2,288,768]{2,1,0:T(8,128)(2,1)S(1)} collective-permute-done((bf16[2,288,768]{2,1,0:T(8,128)(2,1)S(1)}, bf16[2,288,768]{2,1,0:T(8,128)(2,1)S(1)}, u32[]{:S(2)}, u32[]{:S(2)}) %collective-permute-start.31) | collective-permute-done | bytes 884768 | tf_op jit(solution)/shard_map/ppermute | solution.py:55
  130.4 14.2 %collective-permute-done.22.refs_1_ = bf16[8,144,512]{2,1,0:T(8,128)(2,1)} collective-permute-done((bf16[8,144,512]{2,1,0:T(8,128)(2,1)S(1)}, bf16[8,144,512]{2,1,0:T(8,128)(2,1)}, u32[]{:S(2)}, u32[]{:S(2)}) %collective-permute-start.22) | collective-permute-done | bytes 1179680 | tf_op jit(solution)/shard_map/ppermute | solution.py:51
  144.7 3.8 %collective-permute-done.25.refs_3_ = bf16[8,144,512]{2,1,0:T(8,128)(2,1)} collective-permute-done((bf16[8,144,512]{2,1,0:T(8,128)(2,1)S(1)}, bf16[8,144,512]{2,1,0:T(8,128)(2,1)}, u32[]{:S(2)}, u32[]{:S(2)}) %collective-permute-start.25) | collective-permute-done | bytes 1179680 | tf_op jit(solution)/shard_map/ppermute | solution.py:51
  148.5 4.7 %shard_map.94 = (bf16[2,128,2048]{2,1,0:T(8,128)(2,1)}, bf16[2,128,2048]{2,1,0:T(8,128)(2,1)}) custom-call(s32[8]{0:T(128)} %stack.180.scalars, bf16[8,2,144,128]{3,2,1,0:T(8,128)(2,1)} %shard_map.87.weight_ref, bf16[1152,4096]{1,0:T(8,128)(2,1)} %own_ref.7, bf16[1152,4096]{1,0:T(8,128)(2,1)} %collective-permute-done.5.sib_ref), custom_call_target="tpu_custom_call" | custom-call | tf_op jit(solution)/shard_map/pallas_call | solution.py:154
  153.2 3.4 %collective-permute-done.24.refs_2_ = bf16[8,144,512]{2,1,0:T(8,128)(2,1)} collective-permute-done((bf16[8,144,512]{2,1,0:T(8,128)(2,1)S(1)}, bf16[8,144,512]{2,1,0:T(8,128)(2,1)}, u32[]{:S(2)}, u32[]{:S(2)}) %collective-permute-start.24) | collective-permute-done | bytes 1179680 | tf_op jit(solution)/shard_map/ppermute | solution.py:51
  163.8 4.8 %shard_map.95 = (bf16[2,128,2048]{2,1,0:T(8,128)(2,1)}, bf16[2,128,2048]{2,1,0:T(8,128)(2,1)}) custom-call(s32[8]{0:T(128)} %stack.180.scalars, bf16[8,2,144,128]{3,2,1,0:T(8,128)(2,1)} %shard_map.87.weight_ref, bf16[1152,4096]{1,0:T(8,128)(2,1)} %own_ref.7, bf16[1152,4096]{1,0:T(8,128)(2,1)} %collective-permute-done.5.sib_ref), custom_call_target="tpu_custom_call" | custom-call | tf_op jit(solution)/shard_map/pallas_call | solution.py:154
  171.5 13.4 %shard_map.89.near_ref = bf16[8,4,144,512]{3,2,1,0:T(8,128)(2,1)} custom-call(s32[1]{0:T(128)} %bitcast.scalars, bf16[4,288,72]{2,1,0:T(8,128)(2,1)} %and_convert_fusion.spread_ref, bf16[8,144,512]{2,1,0:T(8,128)(2,1)} %bitcast.78, bf16[8,144,512]{2,1,0:T(8,128)(2,1)} %copy-done.7, bf16[8,144,512]{2,1,0:T(8,128)(2,1)} %copy-done.9, ...), custom_call_target="tpu_custom_call" | custom-call | tf_op jit(solution)/shard_map/pallas_call | solution.py:198
  187.0 4.7 %shard_map.93 = (bf16[2,128,2048]{2,1,0:T(8,128)(2,1)}, bf16[2,128,2048]{2,1,0:T(8,128)(2,1)}) custom-call(s32[8]{0:T(128)} %stack.180.scalars, bf16[8,2,144,128]{3,2,1,0:T(8,128)(2,1)} %shard_map.87.weight_ref, bf16[1152,4096]{1,0:T(8,128)(2,1)} %own_ref.7, bf16[1152,4096]{1,0:T(8,128)(2,1)} %collective-permute-done.5.sib_ref), custom_call_target="tpu_custom_call" | custom-call | tf_op jit(solution)/shard_map/pallas_call | solution.py:154
  191.7 4.5 %collective-permute-done.37 = bf16[2,128,2048]{2,1,0:T(8,128)(2,1)} collective-permute-done((bf16[2,128,2048]{2,1,0:T(8,128)(2,1)}, bf16[2,128,2048]{2,1,0:T(8,128)(2,1)}, u32[]{:S(2)}, u32[]{:S(2)}) %collective-permute-start.37) | collective-permute-done | bytes 1048608 | tf_op jit(solution)/shard_map/ppermute | solution.py:51
  206.2 13.5 %shard_map.90.far_ref = bf16[8,4,144,512]{3,2,1,0:T(8,128)(2,1)} custom-call(s32[1]{0:T(128)} %bitcast.scalars, bf16[4,288,72]{2,1,0:T(8,128)(2,1)} %and_convert_fusion.spread_ref, bf16[8,144,512]{2,1,0:T(8,128)(2,1)} %copy-done.13, bf16[8,144,512]{2,1,0:T(8,128)(2,1)} %collective-permute-done.22.refs_1_, ...), custom_call_target="tpu_custom_call" | custom-call | tf_op jit(solution)/shard_map/pallas_call | solution.py:198
  223.0 9.4 %shard_map.91.refs_0_ = f32[4,768,512]{2,1,0:T(8,128)} custom-call(bf16[8,4,144,512]{3,2,1,0:T(8,128)(2,1)} %shard_map.89.near_ref, bf16[8,4,144,512]{3,2,1,0:T(8,128)(2,1)} %shard_map.90.far_ref, bf16[4,288,768]{2,1,0:T(8,128)(2,1)} %bitcast.82, bf16[4,288,768]{2,1,0:T(8,128)(2,1)} %copy-done.5, bf16[2,288,768]{2,1,0:T(8,128)(2,1)} %copy-done.24, ...), custom_call_target="tpu_custom_call" | custom-call | tf_op jit(solution)/shard_map/pallas_call | solution.py:230
  232.4 10.9 %shard_map.92 = f32[4,768,512]{2,1,0:T(8,128)} custom-call(bf16[8,4,144,512]{3,2,1,0:T(8,128)(2,1)} %shard_map.89.near_ref, bf16[8,4,144,512]{3,2,1,0:T(8,128)(2,1)} %shard_map.90.far_ref, bf16[4,288,768]{2,1,0:T(8,128)(2,1)} %copy-done.10, bf16[4,288,768]{2,1,0:T(8,128)(2,1)} %copy-done.3, bf16[2,288,768]{2,1,0:T(8,128)(2,1)} %collective-permute-done.33.low_ref, ...), custom_call_target="tpu_custom_call" | custom-call | tf_op jit(solution)/shard_map/pallas_call | solution.py:230
  (167 shorter events, 78.0 us)
Async XLA Ops:
  0.6 25.4 %collective-permute-start.5 = (bf16[1152,4096]{1,0:T(8,128)(2,1)}, bf16[1152,4096]{1,0:T(8,128)(2,1)}, u32[]{:S(2)}, u32[]{:S(2)}) collective-permute-start(bf16[1152,4096]{1,0:T(8,128)(2,1)} %own_ref.7), channel_id=1, source_target_pairs={{1,0},{0,1},{3,2},{2,3},{5,4},{4,5},{7,6},{6,7},{9,8},{8,9},{11,10... | collective-permute-start | bytes 28311560 | tf_op jit(solution)/shard_map/ppermute | solution.py:51
  37.1 25.2 %collective-permute-start.10 = (bf16[2,128,2048]{2,1,0:T(8,128)(2,1)}, bf16[2,128,2048]{2,1,0:T(8,128)(2,1)S(1)}, u32[]{:S(2)}, u32[]{:S(2)}) collective-permute-start(bf16[2,128,2048]{2,1,0:T(8,128)(2,1)} %get-tuple-element.27), channel_id=1, source_target_pairs={{2,0},{3,1},{4,2},{5,3},{6,4},{7,5},{0,6},{1,7},{10,8},{11,9},{12,... | collective-permute-start | bytes 3145736 | tf_op jit(solution)/shard_map/ppermute | solution.py:51
  37.9 25.4 %collective-permute-start.9 = (bf16[2,128,2048]{2,1,0:T(8,128)(2,1)}, bf16[2,128,2048]{2,1,0:T(8,128)(2,1)}, u32[]{:S(2)}, u32[]{:S(2)}) collective-permute-start(bf16[2,128,2048]{2,1,0:T(8,128)(2,1)} %get-tuple-element.26), channel_id=1, source_target_pairs={{6,0},{7,1},{0,2},{1,3},{2,4},{3,5},{4,6},{5,7},{14,8},{15,9},{8,1... | collective-permute-start | bytes 3145736 | tf_op jit(solution)/shard_map/ppermute | solution.py:51
  53.1 28.0 %collective-permute-start.19 = (bf16[8,144,512]{2,1,0:T(8,128)(2,1)S(1)}, bf16[8,144,512]{2,1,0:T(8,128)(2,1)S(1)}, u32[]{:S(2)}, u32[]{:S(2)}) collective-permute-start(bf16[8,144,512]{2,1,0:T(8,128)(2,1)S(1)} %bitcast.74), channel_id=1, source_target_pairs={{8,0},{9,1},{10,2},{11,3},{12,4},{13,5},{14,6},{15,7},{0,8},{1,9},... | collective-permute-start | bytes 3538952 | tf_op jit(solution)/shard_map/ppermute | solution.py:51
  55.9 40.6 %collective-permute-start.20 = (bf16[4,288,768]{2,1,0:T(8,128)(2,1)S(1)}, bf16[4,288,768]{2,1,0:T(8,128)(2,1)S(1)}, u32[]{:S(2)}, u32[]{:S(2)}) collective-permute-start(bf16[4,288,768]{2,1,0:T(8,128)(2,1)S(1)} %bitcast.79), channel_id=1, source_target_pairs={{32,0},{48,16},{64,32},{80,48},{96,64},{112,80},{0,96},{16,112},{3... | collective-permute-start | bytes 5308424 | tf_op jit(solution)/shard_map/ppermute | solution.py:55
  56.5 41.2 %collective-permute-start.21 = (bf16[4,288,768]{2,1,0:T(8,128)(2,1)S(1)}, bf16[4,288,768]{2,1,0:T(8,128)(2,1)S(1)}, u32[]{:S(2)}, u32[]{:S(2)}) collective-permute-start(bf16[4,288,768]{2,1,0:T(8,128)(2,1)S(1)} %bitcast.80), channel_id=1, source_target_pairs={{96,0},{112,16},{0,32},{16,48},{32,64},{48,80},{64,96},{80,112},{9... | collective-permute-start | bytes 5308424 | tf_op jit(solution)/shard_map/ppermute | solution.py:55
  63.3 26.9 %collective-permute-start.11 = (bf16[8,144,512]{2,1,0:T(8,128)(2,1)S(1)}, bf16[8,144,512]{2,1,0:T(8,128)(2,1)S(1)}, u32[]{:S(2)}, u32[]{:S(2)}) collective-permute-start(bf16[8,144,512]{2,1,0:T(8,128)(2,1)S(1)} %bitcast.75), channel_id=1, source_target_pairs={{2,0},{3,1},{4,2},{5,3},{6,4},{7,5},{0,6},{1,7},{10,8},{11,9},{12,... | collective-permute-start | bytes 3538952 | tf_op jit(solution)/shard_map/ppermute | solution.py:51
  63.3 26.9 %collective-permute-start.13 = (bf16[8,144,512]{2,1,0:T(8,128)(2,1)S(1)}, bf16[8,144,512]{2,1,0:T(8,128)(2,1)S(1)}, u32[]{:S(2)}, u32[]{:S(2)}) collective-permute-start(bf16[8,144,512]{2,1,0:T(8,128)(2,1)S(1)} %bitcast.76), channel_id=1, source_target_pairs={{6,0},{7,1},{0,2},{1,3},{2,4},{3,5},{4,6},{5,7},{14,8},{15,9},{8,1... | collective-permute-start | bytes 3538952 | tf_op jit(solution)/shard_map/ppermute | solution.py:51
  81.1 41.2 %collective-permute-start.23 = (bf16[4,288,768]{2,1,0:T(8,128)(2,1)S(1)}, bf16[4,288,768]{2,1,0:T(8,128)(2,1)S(1)}, u32[]{:S(2)}, u32[]{:S(2)}) collective-permute-start(bf16[4,288,768]{2,1,0:T(8,128)(2,1)S(1)} %bitcast.81), channel_id=1, source_target_pairs={{16,0},{0,16},{48,32},{32,48},{80,64},{64,80},{112,96},{96,112},{1... | collective-permute-start | bytes 5308424 | tf_op jit(solution)/shard_map/ppermute | solution.py:55
  117.8 26.8 %collective-permute-start.22 = (bf16[8,144,512]{2,1,0:T(8,128)(2,1)S(1)}, bf16[8,144,512]{2,1,0:T(8,128)(2,1)}, u32[]{:S(2)}, u32[]{:S(2)}) collective-permute-start(bf16[8,144,512]{2,1,0:T(8,128)(2,1)S(1)} %collective-permute-done.19.refs_0_), channel_id=1, source_target_pairs={{2,0},{3,1},{4,2},{5,3},{6,4},{7,5},{0,6},{1,7},{10,8},{11,9},{12,... | collective-permute-start | bytes 3538952 | tf_op jit(solution)/shard_map/ppermute | solution.py:51
  122.3 26.2 %collective-permute-start.25 = (bf16[8,144,512]{2,1,0:T(8,128)(2,1)S(1)}, bf16[8,144,512]{2,1,0:T(8,128)(2,1)}, u32[]{:S(2)}, u32[]{:S(2)}) collective-permute-start(bf16[8,144,512]{2,1,0:T(8,128)(2,1)S(1)} %collective-permute-done.19.refs_0_), channel_id=1, source_target_pairs={{6,0},{7,1},{0,2},{1,3},{2,4},{3,5},{4,6},{5,7},{14,8},{15,9},{8,1... | collective-permute-start | bytes 3538952 | tf_op jit(solution)/shard_map/ppermute | solution.py:51
  129.7 26.9 %collective-permute-start.24 = (bf16[8,144,512]{2,1,0:T(8,128)(2,1)S(1)}, bf16[8,144,512]{2,1,0:T(8,128)(2,1)}, u32[]{:S(2)}, u32[]{:S(2)}) collective-permute-start(bf16[8,144,512]{2,1,0:T(8,128)(2,1)S(1)} %constant_dynamic-update-slice_fusion.refs_2_), channel_id=1, source_target_pairs={{8,0},{9,1},{10,2},{11,3},{12,4},{13,5},{14,6},{15,7},{0,8},{1,9},... | collective-permute-start | bytes 3538952 | tf_op jit(solution)/shard_map/ppermute | solution.py:51
  129.7 30.0 %collective-permute-start.17 = (bf16[8,144,512]{2,1,0:T(8,128)(2,1)S(1)}, bf16[8,144,512]{2,1,0:T(8,128)(2,1)S(1)}, u32[]{:S(2)}, u32[]{:S(2)}) collective-permute-start(bf16[8,144,512]{2,1,0:T(8,128)(2,1)S(1)} %constant_dynamic-update-slice_fusion.refs_2_), channel_id=1, source_target_pairs={{1,0},{0,1},{3,2},{2,3},{5,4},{4,5},{7,6},{6,7},{9,8},{8,9},{11,10... | collective-permute-start | bytes 3538952 | tf_op jit(solution)/shard_map/ppermute | solution.py:51
  129.9 30.9 %collective-permute-start.26 = (bf16[8,144,512]{2,1,0:T(8,128)(2,1)S(1)}, bf16[8,144,512]{2,1,0:T(8,128)(2,1)S(1)}, u32[]{:S(2)}, u32[]{:S(2)}) collective-permute-start(bf16[8,144,512]{2,1,0:T(8,128)(2,1)S(1)} %collective-permute-done.19.refs_0_), channel_id=1, source_target_pairs={{1,0},{0,1},{3,2},{2,3},{5,4},{4,5},{7,6},{6,7},{9,8},{8,9},{11,10... | collective-permute-start | bytes 3538952 | tf_op jit(solution)/shard_map/ppermute | solution.py:51
  156.6 28.2 %collective-permute-start.28 = (bf16[8,144,512]{2,1,0:T(8,128)(2,1)}, bf16[8,144,512]{2,1,0:T(8,128)(2,1)}, u32[]{:S(2)}, u32[]{:S(2)}) collective-permute-start(bf16[8,144,512]{2,1,0:T(8,128)(2,1)} %collective-permute-done.24.refs_2_), channel_id=1, source_target_pairs={{1,0},{0,1},{3,2},{2,3},{5,4},{4,5},{7,6},{6,7},{9,8},{8,9},{11,10... | collective-permute-start | bytes 3538952 | tf_op jit(solution)/shard_map/ppermute | solution.py:51
  159.7 27.3 %collective-permute-start.36 = (bf16[2,128,2048]{2,1,0:T(8,128)(2,1)}, bf16[2,128,2048]{2,1,0:T(8,128)(2,1)}, u32[]{:S(2)}, u32[]{:S(2)}) collective-permute-start(bf16[2,128,2048]{2,1,0:T(8,128)(2,1)} %add_convert_fusion.1), channel_id=1, source_target_pairs={{6,0},{7,1},{0,2},{1,3},{2,4},{3,5},{4,6},{5,7},{14,8},{15,9},{8,1... | collective-permute-start | bytes 3145736 | tf_op jit(solution)/shard_map/ppermute | solution.py:51
  160.7 41.1 %collective-permute-start.32 = (bf16[4,288,768]{2,1,0:T(8,128)(2,1)S(1)}, bf16[4,288,768]{2,1,0:T(8,128)(2,1)S(1)}, u32[]{:S(2)}, u32[]{:S(2)}) collective-permute-start(bf16[4,288,768]{2,1,0:T(8,128)(2,1)S(1)} %copy-done.11), channel_id=1, source_target_pairs={{32,0},{48,16},{64,32},{80,48},{96,64},{112,80},{0,96},{16,112},{3... | collective-permute-start | bytes 5308424 | tf_op jit(solution)/shard_map/ppermute | solution.py:55
  161.9 43.3 %collective-permute-start.34 = (bf16[4,288,768]{2,1,0:T(8,128)(2,1)S(1)}, bf16[4,288,768]{2,1,0:T(8,128)(2,1)S(1)}, u32[]{:S(2)}, u32[]{:S(2)}) collective-permute-start(bf16[4,288,768]{2,1,0:T(8,128)(2,1)S(1)} %copy-done.11), channel_id=1, source_target_pairs={{96,0},{112,16},{0,32},{16,48},{32,64},{48,80},{64,96},{80,112},{9... | collective-permute-start | bytes 5308424 | tf_op jit(solution)/shard_map/ppermute | solution.py:55
  168.6 27.6 %collective-permute-start.37 = (bf16[2,128,2048]{2,1,0:T(8,128)(2,1)}, bf16[2,128,2048]{2,1,0:T(8,128)(2,1)}, u32[]{:S(2)}, u32[]{:S(2)}) collective-permute-start(bf16[2,128,2048]{2,1,0:T(8,128)(2,1)} %get-tuple-element.39), channel_id=1, source_target_pairs={{2,0},{3,1},{4,2},{5,3},{6,4},{7,5},{0,6},{1,7},{10,8},{11,9},{12,... | collective-permute-start | bytes 3145736 | tf_op jit(solution)/shard_map/ppermute | solution.py:51
  184.9 34.9 %collective-permute-start.39 = (bf16[2,128,2048]{2,1,0:T(8,128)(2,1)}, bf16[2,128,2048]{2,1,0:T(8,128)(2,1)S(1)}, u32[]{:S(2)}, u32[]{:S(2)}) collective-permute-start(bf16[2,128,2048]{2,1,0:T(8,128)(2,1)} %get-tuple-element.42), channel_id=1, source_target_pairs={{6,0},{7,1},{0,2},{1,3},{2,4},{3,5},{4,6},{5,7},{14,8},{15,9},{8,1... | collective-permute-start | bytes 3145736 | tf_op jit(solution)/shard_map/ppermute | solution.py:51
  187.0 32.7 %collective-permute-start.40 = (bf16[2,128,2048]{2,1,0:T(8,128)(2,1)S(1)}, bf16[2,128,2048]{2,1,0:T(8,128)(2,1)}, u32[]{:S(2)}, u32[]{:S(2)}) collective-permute-start(bf16[2,128,2048]{2,1,0:T(8,128)(2,1)S(1)} %add_convert_fusion), channel_id=1, source_target_pairs={{2,0},{3,1},{4,2},{5,3},{6,4},{7,5},{0,6},{1,7},{10,8},{11,9},{12,... | collective-permute-start | bytes 3145736 | tf_op jit(solution)/shard_map/ppermute | solution.py:51
  198.6 22.9 %collective-permute-start.38 = (bf16[128,2048]{1,0:T(8,128)(2,1)}, bf16[128,2048]{1,0:T(8,128)(2,1)S(1)}, u32[]{:S(2)}, u32[]{:S(2)}) collective-permute-start(bf16[128,2048]{1,0:T(8,128)(2,1)} %fusion.5), channel_id=1, source_target_pairs={{8,0},{9,1},{10,2},{11,3},{12,4},{13,5},{14,6},{15,7},{0,8},{1,9},... | collective-permute-start | bytes 1572872 | tf_op jit(solution)/shard_map/ppermute | solution.py:51
  202.9 29.6 %collective-permute-start.33 = (bf16[2,288,768]{2,1,0:T(8,128)(2,1)}, bf16[2,288,768]{2,1,0:T(8,128)(2,1)}, u32[]{:S(2)}, u32[]{:S(2)}) collective-permute-start(bf16[2,288,768]{2,1,0:T(8,128)(2,1)} %slice.100), channel_id=1, source_target_pairs={{32,0},{48,16},{64,32},{80,48},{96,64},{112,80},{0,96},{16,112},{3... | collective-permute-start | bytes 2654216 | tf_op jit(solution)/shard_map/ppermute | solution.py:55
  206.2 26.2 %collective-permute-start.35 = (bf16[2,288,768]{2,1,0:T(8,128)(2,1)}, bf16[2,288,768]{2,1,0:T(8,128)(2,1)}, u32[]{:S(2)}, u32[]{:S(2)}) collective-permute-start(bf16[2,288,768]{2,1,0:T(8,128)(2,1)} %slice.101), channel_id=1, source_target_pairs={{96,0},{112,16},{0,32},{16,48},{32,64},{48,80},{64,96},{80,112},{9... | collective-permute-start | bytes 2654216 | tf_op jit(solution)/shard_map/ppermute | solution.py:55
  (46 other events, 794.6 us)

commit v2 on v1

v2 whole, which is shorter than its diff:
```python
import functools

import jax
import jax.numpy as jnp
from jax import lax
from jax.experimental import pallas as pl
from jax.experimental.pallas import tpu as pltpu
from jax.sharding import PartitionSpec as P

E = 4
CAP = 18
SLOT = E * CAP
PAIR = 2 * SLOT
TOK = 128
TOP = 8
D = 4096
HALF = D // 2
COLS = 512
FFW = 768
NDP = 8
NEX = 16
X = 4
ROWS = NEX * CAP
LONG = TOK + 16
QUAD = 4
BATCH = 4

VMEM = 56 * 1024 * 1024


def ex_perm(dzl, dx, dc):
    pairs = []
    for zl in range(2):
        for x in range(X):
            for c in range(2):
                src = ((zl ^ dzl) * X + (x + dx) % X) * 2 + (c ^ dc)
                pairs.append((src, (zl * X + x) * 2 + c))
    return pairs


def dp_perm(dy, dzh):
    pairs = []
    for y in range(4):
        for zh in range(2):
            pairs.append((((y + dy) % 4) * 2 + (zh ^ dzh), y * 2 + zh))
    return pairs


def ex_from(value, dzl, dx, dc):
    return lax.ppermute(value, "expert", ex_perm(dzl, dx, dc))


def dp_from(value, dy, dzh):
    return lax.ppermute(value, "dp", dp_perm(dy, dzh))


def slot_weights(blocks):
    slot = lax.broadcasted_iota(jnp.int32, (SLOT, TOK), 0)
    expert = (
        (slot >= CAP).astype(jnp.int32)
        + (slot >= 2 * CAP).astype(jnp.int32)
        + (slot >= 3 * CAP).astype(jnp.int32)
    )
    place = (slot - CAP * expert).astype(jnp.float32)
    gates = []
    for lines, first_expert in blocks:
        name = (expert + first_expert).astype(jnp.float32)
        gate = jnp.zeros((SLOT, TOK), jnp.float32)
        for k in range(TOP):
            gate = jnp.where(lines[k] == name, lines[TOP + k], gate)
        gates.append(gate)
    earlier = (
        lax.broadcasted_iota(jnp.int32, (TOK, TOK), 0)
        < lax.broadcasted_iota(jnp.int32, (TOK, TOK), 1)
    ).astype(jnp.bfloat16)
    named = jnp.concatenate([(gate > 0.0).astype(jnp.float32) for gate in gates], axis=0)
    rank = jnp.dot(named.astype(jnp.bfloat16), earlier, preferred_element_type=jnp.float32)
    return [
        jnp.where(rank[i * SLOT : (i + 1) * SLOT] == place, gate, 0.0)
        for i, gate in enumerate(gates)
    ]


def cut_columns_kernel(targets, grad_ref, meta_ref, *out_refs):
    table = meta_ref[2 * TOP :, :].astype(jnp.bfloat16)
    table = jnp.concatenate([table, jnp.zeros((2 * TOP, COLS - TOK), jnp.bfloat16)], axis=1)
    outs = [ref.at[dy] for ref in out_refs for dy in range(4)]
    for i, out in enumerate(outs):
        at = pl.multiple_of(targets[i] * COLS, COLS)
        out[:TOK, :] = grad_ref[:, pl.ds(at, COLS)]
        out[TOK:, :] = table


def cut_columns(targets, grad, meta):
    shapes = [(4, LONG, COLS)] * 2
    return pl.pallas_call(
        cut_columns_kernel,
        grid_spec=pltpu.PrefetchScalarGridSpec(
            num_scalar_prefetch=1,
            grid=(1,),
            in_specs=[
                pl.BlockSpec((TOK, D), lambda i, s: (0, 0)),
                pl.BlockSpec((4 * TOP, TOK), lambda i, s: (0, 0)),
            ],
            out_specs=[pl.BlockSpec(s, lambda i, _, n=len(s): (0,) * n) for s in shapes],
        ),
        out_shape=[jax.ShapeDtypeStruct(s, jnp.bfloat16) for s in shapes],
        compiler_params=pltpu.CompilerParams(vmem_limit_bytes=VMEM),
    )(targets, grad, meta)


def return_route_kernel(scalars, meta_ref, out_ref):
    core = scalars[0]
    blocks = []
    for i in range(8):
        lines = [meta_ref[i, k : k + 1, :] for k in range(2 * TOP)]
        blocks += [(lines, scalars[1]), (lines, scalars[2])]
    for n, gate in enumerate(slot_weights(blocks)):
        none = jnp.zeros_like(gate)
        both = jnp.concatenate(
            [jnp.where(core == 0, gate, none), jnp.where(core == 1, gate, none)], axis=0
        )
        out_ref[n // 2, n % 2] = both.astype(jnp.bfloat16)


def return_route(scalars, meta):
    return pl.pallas_call(
        return_route_kernel,
        grid_spec=pltpu.PrefetchScalarGridSpec(
            num_scalar_prefetch=1,
            grid=(1,),
            in_specs=[pl.BlockSpec((8, 2 * TOP, TOK), lambda i, s: (0, 0, 0))],
            out_specs=pl.BlockSpec((8, 2, PAIR, TOK), lambda i, s: (0, 0, 0, 0)),
        ),
        out_shape=jax.ShapeDtypeStruct((8, 2, PAIR, TOK), jnp.bfloat16),
        compiler_params=pltpu.CompilerParams(vmem_limit_bytes=VMEM),
    )(scalars, meta)


def combine_kernel(scalars, weight_ref, own_ref, sib_ref, *out_refs, outs):
    chunk = 1024
    for at in range(0, D, chunk):
        total = jnp.zeros((TOK, chunk), jnp.float32)
        for j, rows in enumerate((own_ref, sib_ref)):
            total += lax.dot_general(
                weight_ref[0, j],
                rows[:, at : at + chunk],
                (((0,), (0,)), ((), ())),
                preferred_element_type=jnp.float32,
            )
        for (low, high), ref in zip(outs, out_refs):
            if low <= at < high:
                ref[0, :, at - low : at - low + chunk] = total.astype(jnp.bfloat16)


def combine(pairs, weights, own, sib, first, steps, outs):
    out_specs = [pl.BlockSpec((1, TOK, high - low), lambda i, s: (i, 0, 0)) for low, high in outs]
    return pl.pallas_call(
        functools.partial(combine_kernel, outs=outs),
        grid_spec=pltpu.PrefetchScalarGridSpec(
            num_scalar_prefetch=1,
            grid=(steps,),
            in_specs=[
                pl.BlockSpec((1, 2, PAIR, TOK), lambda i, s: (first + i, 0, 0, 0)),
                pl.BlockSpec((PAIR, D), lambda i, s: (s[first + i], 0)),
                pl.BlockSpec((PAIR, D), lambda i, s: (s[first + i], 0)),
            ],
            out_specs=out_specs,
        ),
        out_shape=[
            jax.ShapeDtypeStruct((steps, TOK, high - low), jnp.bfloat16) for low, high in outs
        ],
        compiler_params=pltpu.CompilerParams(vmem_limit_bytes=VMEM),
    )(pairs, weights, own, sib)


def sent_kernel(scalars, order_ref, *refs):
    tok_refs, out_refs = refs[:QUAD], refs[QUAD:]
    tokens = jnp.concatenate([ref[0, :TOK, :] for ref in tok_refs], axis=0)
    blocks = []
    for j in range(2):
        for ref in tok_refs:
            table = ref[0, TOK:, :TOK].astype(jnp.float32)
            blocks.append(([table[k : k + 1, :] for k in range(2 * TOP)], scalars[j]))
    gates = slot_weights(blocks)
    none = jnp.zeros((SLOT, TOK), jnp.float32)
    for j, out_ref in enumerate(out_refs):
        route = [
            jnp.concatenate(
                [gates[j * QUAD + i] if i == n else none for n in range(QUAD)], axis=1
            )
            for i in range(QUAD)
        ]
        route = jnp.concatenate(route, axis=0).astype(jnp.bfloat16)
        route = jnp.dot(order_ref[...], route, preferred_element_type=jnp.float32)
        sent = jnp.dot(route.astype(jnp.bfloat16), tokens, preferred_element_type=jnp.float32)
        for e in range(E):
            out_ref[0, e] = sent[e * SLOT : (e + 1) * SLOT, :].astype(jnp.bfloat16)


def build_sent(scalars, order, tokens):
    rows = (NDP, E, SLOT, COLS)
    return pl.pallas_call(
        sent_kernel,
        grid_spec=pltpu.PrefetchScalarGridSpec(
            num_scalar_prefetch=1,
            grid=(NDP,),
            in_specs=[pl.BlockSpec((QUAD * SLOT, QUAD * SLOT), lambda g, s: (0, 0))]
            + [pl.BlockSpec((1, LONG, COLS), lambda g, s: (g, 0, 0)) for _ in range(QUAD)],
            out_specs=[pl.BlockSpec((1,) + rows[1:], lambda g, s: (g, 0, 0, 0))] * 2,
        ),
        out_shape=[jax.ShapeDtypeStruct(rows, jnp.bfloat16)] * 2,
        compiler_params=pltpu.CompilerParams(vmem_limit_bytes=VMEM),
        cost_estimate=pl.CostEstimate(
            flops=14_000_000_000, bytes_accessed=15_000_000, transcendentals=0
        ),
    )(scalars, order, *tokens)


def weight_kernel(*refs, counts):
    sent_refs, refs = refs[:4], refs[4:]
    hidden = []
    for count in counts:
        part, refs = refs[:count], refs[count:]
        if count == 2:
            hidden.append(jnp.where(pl.program_id(0) < E // 2, part[0][0], part[1][0]))
        else:
            hidden.append(part[0][0])
    hidden = jnp.concatenate(hidden, axis=0)
    sent = [ref[g, 0].astype(jnp.float32) for g in range(BATCH) for ref in sent_refs]
    sent = jnp.concatenate(sent, axis=0).astype(jnp.bfloat16)
    total = lax.dot_general(
        hidden, sent, (((0,), (0,)), ((), ())), preferred_element_type=jnp.float32
    )
    if len(refs) > 1:
        total += refs[0][0]
    refs[-1][0] = total


def weight_grad(sents, batch, sources, before):
    result = pl.BlockSpec((1, FFW, COLS), lambda e: (e, 0, 0))
    whole = pl.BlockSpec((1, ROWS, FFW), lambda e: (e, 0, 0))
    halves = [
        pl.BlockSpec((1, ROWS, FFW), lambda e: (jnp.minimum(e, E // 2 - 1), 0, 0)),
        pl.BlockSpec((1, ROWS, FFW), lambda e: (jnp.maximum(e - E // 2, 0), 0, 0)),
    ]
    specs = [spec for s in sources for spec in (halves if len(s) == 2 else [whole])]
    return pl.pallas_call(
        functools.partial(weight_kernel, counts=tuple(len(s) for s in sources)),
        grid=(E,),
        in_specs=[pl.BlockSpec((BATCH, 1, SLOT, COLS), lambda e: (batch, e, 0, 0))] * 4
        + specs
        + [result] * len(before),
        out_specs=result,
        out_shape=jax.ShapeDtypeStruct((E, FFW, COLS), jnp.float32),
        compiler_params=pltpu.CompilerParams(vmem_limit_bytes=VMEM),
        cost_estimate=pl.CostEstimate(
            flops=11_000_000_000, bytes_accessed=20_000_000, transcendentals=0
        ),
    )(*sents, *[a for s in sources for a in s], *before)


def local(
    grad_next, gate_next, expert_ids_next, hidden_next, slot_grads, gate_prev, expert_ids_prev
):
    me = lax.axis_index("expert")
    zl, x, c = me // (2 * X), (me // 2) % X, me % 2
    dp = lax.axis_index("dp")
    y, zh = dp // 2, dp % 2
    first = (me * E).astype(jnp.int32)

    def after(value, *earlier):
        return lax.optimization_barrier((value, earlier))[0]

    meta = jnp.concatenate(
        [
            expert_ids_prev.astype(jnp.float32),
            gate_prev,
            expert_ids_next.astype(jnp.float32),
            gate_next,
        ],
        axis=1,
    ).T

    targets = [((y - dy) % 4) * 2 + z for z in (zh, 1 - zh) for dy in range(4)]
    same, other = cut_columns(jnp.stack(targets).astype(jnp.int32), grad_next, meta)
    other = dp_from(other, 0, 1)

    meta = meta[: 2 * TOP]
    meta = jnp.stack([meta, ex_from(meta, 1, 0, 0)])
    meta = jnp.stack([meta] + [ex_from(meta, 0, dx, 0) for dx in (1, 2, 3)])
    meta_prev = meta.reshape(8, 2 * TOP, TOK)

    sibling = ex_from(slot_grads, 0, 0, 1)
    weights = return_route(
        jnp.stack([c, first, (me ^ 1) * E]).astype(jnp.int32), meta_prev
    )
    pairs = jnp.stack(
        [(zl ^ dzl) * X + (x + dx) % X for dx in range(X) for dzl in range(2)]
    ).astype(jnp.int32)
    halves = [(0, HALF), (HALF, D)]

    def part(dx):
        return combine(pairs, weights, slot_grads, sibling, 2 * dx, 2, halves)

    def add(*values):
        return sum(v.astype(jnp.float32) for v in values).astype(jnp.bfloat16)

    blocks = jnp.stack(
        [
            ((zl ^ dzl) * X + (x + dx) % X) * 2 + (c ^ dc)
            for dzl in range(2)
            for dc in range(2)
            for dx in range(X)
        ]
    ).reshape(1, NEX, 1)
    source = (
        blocks * SLOT
        + jnp.arange(E, dtype=jnp.int32)[:, None, None] * CAP
        + jnp.arange(CAP, dtype=jnp.int32)[None, None, :]
    ).reshape(-1)
    move = (source[:, None] == jnp.arange(NEX * SLOT, dtype=jnp.int32)[None, :]).astype(
        jnp.bfloat16
    )
    mine = jnp.dot(move, hidden_next, preferred_element_type=jnp.float32).astype(jnp.bfloat16)
    mine = mine.reshape(E, ROWS, FFW)

    left, right = part(2)
    both = after(jnp.stack([same, other], axis=1), left, right)
    own = [both[0]] + [dp_from(both[dy], dy, 0) for dy in (1, 2, 3)]
    left, right = ex_from(left, 0, 3, 0), ex_from(right, 0, 1, 0)
    up, down, here = part(1), part(3), part(0)
    own = after(own, left, right, *up, *down, *here)
    own = jnp.stack(own, axis=1).reshape(NDP, LONG, COLS)
    up = [add(up[0], left), up[1]]
    down = [down[0], add(down[1], right)]

    def to_sides(zero):
        return dp_from(zero, 1, 0), dp_from(zero, 3, 0)

    mine_low, mine_high = mine[: E // 2], mine[E // 2 :]
    low_near = to_sides(after(mine_low, own))
    high_near = to_sides(after(mine_high, *low_near))
    near_onward = after((low_near[0], high_near[1]), *low_near, *high_near)
    near_onward = dp_from(near_onward[0], 1, 0), dp_from(near_onward[1], 3, 0)

    over = ex_from(own, 1, 0, 0)
    across_low = dp_from(after(mine_low, over), 0, 1)
    near = [own, ex_from(own, 0, 1, 0), None, ex_from(own, 0, 3, 0)]
    near[2] = jnp.concatenate(
        [
            ex_from(after(near[1][:BATCH], over, *up, *down, *low_near), 0, 1, 0),
            ex_from(after(near[3][BATCH:], over, *up, *down, *low_near), 0, 3, 0),
        ]
    )
    to = jnp.arange(QUAD * SLOT, dtype=jnp.int32)
    block_row = to % SLOT // CAP * SLOT + to // SLOT * CAP + to % CAP
    order = (block_row[:, None] == to[None, :]).astype(jnp.bfloat16)
    both_first = jnp.stack([first, (me ^ 1) * E]).astype(jnp.int32)

    def slot_rows(tokens):
        mine_rows, theirs = build_sent(both_first, order, tokens)
        return [mine_rows, ex_from(theirs, 0, 0, 1)]

    sents = slot_rows(after(near, *high_near))
    over_late = after(over, near[2])
    far = [
        over,
        ex_from(over_late, 0, 1, 0),
        ex_from(after(near[2], across_low), 1, 0, 0),
        ex_from(over_late, 0, 3, 0),
    ]

    across_high = dp_from(after(mine_high, far[2]), 0, 1)
    low_far = to_sides(after(across_low, *near_onward))
    high_far = to_sides(after(across_high, *low_far))
    far_onward = after((low_far[0], high_far[1]), *low_far, *high_far)
    far_onward = dp_from(far_onward[0], 1, 0), dp_from(far_onward[1], 3, 0)

    crossed = []
    gates = [(far[1], far[3], *near_onward), low_far]
    for i in range(2):
        if i:
            sents = sents + slot_rows(far)
        u = ex_from(after(up[i], *gates[i], *sents), 0, 3, 0)
        d = ex_from(after(down[i], *gates[i], *sents), 0, 1, 0)
        gates[1] += (u, d)
        side = add(here[i][1], u[1], d[1])
        if i:
            sources = [(mine_low, mine_high), *zip(low_near, high_near)]
            sources.insert(2, near_onward)
            down_grad = weight_grad(sents, 0, sources, [])
            side = after(side, down_grad, *high_far)
        side = ex_from(side, 1, 0, 0)
        crossed.append(add(here[i][0], u[0], d[0], side))
    input_grad = jnp.concatenate(crossed, axis=1)
    sources = [(across_low, across_high), *zip(low_far, high_far)]
    sources.insert(2, far_onward)
    down_grad = weight_grad(sents, 1, sources, [down_grad])
    return down_grad, input_grad


def solution(mesh):
    rows = P(("dp", "expert"), None)
    return jax.shard_map(
        local,
        mesh=mesh,
        in_specs=(rows,) * 7,
        out_specs=(P("expert", None, "dp"), rows),
        check_vma=False,
    )
```

time: 247 us -> 236 us (0.955)
  waiting for transfers between devices: 103 us -> 89.3 us
  starting transfers between devices: 40.7 us -> 51.1 us
  other arithmetic: 18.7 us -> 13.9 us
  Pallas kernels: 72 us -> 68.8 us
    ppermute x29 -> x23, waiting for transfers between devices: 62.1 us -> 29.1 us  [ex_from(): return lax.ppermute(value, 'expert', ex_perm(dzl, dx, dc))]
    ppermute x13 -> x18, waiting for transfers between devices: 41.3 us -> 60.3 us  [dp_from(): return lax.ppermute(value, 'dp', dp_perm(dy, dzh))]
    ppermute x29 -> x23, starting transfers between devices: 20.3 us -> 27 us  [ex_from(): return lax.ppermute(value, 'expert', ex_perm(dzl, dx, dc))]
    convert_element_type x6, other arithmetic: 11.5 us -> 5.35 us  [add(): return sum((v.astype(jnp.float32) for v in values)).astype(jnp.bfloat16)]
    ppermute x13 -> x18, starting transfers between devices: 20.3 us -> 24.1 us  [dp_from(): return lax.ppermute(value, 'dp', dp_perm(dy, dzh))]
    pallas_call x2, Pallas kernels: 26.9 us -> 23.7 us  [build_sent(): pl.pallas_call(sent_kernel, grid_spec=pltpu.PrefetchScalarGridSpec(num_sc...]
  transfers between devices with their start and end apart: 42 -> 41, of which waited for: 19 -> 17; matrix products, arithmetic and copies ran while one was open for 9% -> 7% of each run, Pallas kernels for 27% -> 29%
where the time goes in v2:
time: 236 us; the launch traced here: 235 us
  waiting for transfers between devices  89.3 us (38%)
  Pallas kernels  68.8 us (29%)
  starting transfers between devices  51.1 us (22%)
  other arithmetic  13.9 us (6%)
  local copies, waits for them, and re-layouts  8.17 us (3%)
  matrix products  2.6 us (1%)
    ppermute x18, waiting for transfers between devices, dp_from(): return lax.ppermute(value, 'dp', dp_perm(dy, dzh))  60.3 us
    ppermute x23, waiting for transfers between devices, ex_from(): return lax.ppermute(value, 'expert', ex_perm(dzl, dx, dc))  29.1 us
    ppermute x23, starting transfers between devices, ex_from(): return lax.ppermute(value, 'expert', ex_perm(dzl, dx, dc))  27 us
    ppermute x18, starting transfers between devices, dp_from(): return lax.ppermute(value, 'dp', dp_perm(dy, dzh))  24.1 us
    pallas_call x2, Pallas kernels, build_sent(): pl.pallas_call(sent_kernel, grid_spec=pltpu.PrefetchScalarGridSpec(num_sc...  23.7 us
    pallas_call x2, Pallas kernels, weight_grad(): pl.pallas_call(functools.partial(weight_kernel, counts=tuple((len(s) for...  20.6 us
    pallas_call x4, Pallas kernels, combine(): pl.pallas_call(functools.partial(combine_kernel, outs=outs), grid_spec=pl...  18.8 us
    convert_element_type x6, other arithmetic, add(): return sum((v.astype(jnp.float32) for v in values)).astype(jnp.bfloat16)  5.35 us
  transfers between devices with their start and end apart: 41, of which 17 were waited for; matrix products, arithmetic and copies ran while one was open for 7% of the time, Pallas kernels for 29%

profile of v2, /device:TPU:6, one launch (start us, length us, event | category | flops | bytes accessed | tf_op | source)
XLA Modules:
  0.0 235.0 jit_solution(10141306114239850411)
XLA Ops:
  5.5 3.0 %shard_map.86 = (bf16[4,144,512]{2,1,0:T(8,128)(2,1)}, bf16[4,144,512]{2,1,0:T(8,128)(2,1)}) custom-call(s32[8]{0:T(128)} %stack.181.targets, bf16[128,4096]{1,0:T(8,128)(2,1)} %grad_ref.1, f32[32,128]{1,0:T(8,128)} %copy-done.12), custom_call_target="tpu_custom_call" | custom-call | tf_op jit(solution)/shard_map/pallas_call | solution.py:96
  8.5 3.6 %collective-permute-start = (bf16[4,144,512]{2,1,0:T(8,128)(2,1)}, bf16[4,144,512]{2,1,0:T(8,128)(2,1)}, u32[]{:S(2)}, u32[]{:S(2)}) collective-permute-start(bf16[4,144,512]{2,1,0:T(8,128)(2,1)} %get-tuple-element.45), channel_id=1, source_target_pairs={{16,0},{0,16},{48,32},{32,48},{80,64},{64,80},{112,96},{96,112},{1... | collective-permute-start | bytes 1769480 | tf_op jit(solution)/shard_map/ppermute | solution.py:54
  21.8 4.8 %shard_map.88 = (bf16[2,128,2048]{2,1,0:T(8,128)(2,1)}, bf16[2,128,2048]{2,1,0:T(8,128)(2,1)}) custom-call(s32[8]{0:T(128)} %stack.193.scalars, bf16[8,2,144,128]{3,2,1,0:T(8,128)(2,1)} %shard_map.87.weight_ref, bf16[1152,4096]{1,0:T(8,128)(2,1)} %own_ref.7, bf16[1152,4096]{1,0:T(8,128)(2,1)} %collective-permute-done.5.sib_ref), custom_call_target="tpu_custom_call" | custom-call | tf_op jit(solution)/shard_map/pallas_call | solution.py:158
  31.9 3.0 %collective-permute-start.6 = (bf16[2,144,512]{2,1,0:T(8,128)(2,1)}, bf16[2,144,512]{2,1,0:T(8,128)(2,1)S(1)}, u32[]{:S(2)}, u32[]{:S(2)}) collective-permute-start(bf16[2,144,512]{2,1,0:T(8,128)(2,1)} %get-tuple-element.89), channel_id=1, source_target_pairs={{32,0},{48,16},{64,32},{80,48},{96,64},{112,80},{0,96},{16,112},{3... | collective-permute-start | bytes 884744 | tf_op jit(solution)/shard_map/ppermute | solution.py:54
  37.5 4.7 %shard_map.89 = (bf16[2,128,2048]{2,1,0:T(8,128)(2,1)}, bf16[2,128,2048]{2,1,0:T(8,128)(2,1)}) custom-call(s32[8]{0:T(128)} %stack.193.scalars, bf16[8,2,144,128]{3,2,1,0:T(8,128)(2,1)} %shard_map.87.weight_ref, bf16[1152,4096]{1,0:T(8,128)(2,1)} %own_ref.7, bf16[1152,4096]{1,0:T(8,128)(2,1)} %collective-permute-done.5.sib_ref), custom_call_target="tpu_custom_call" | custom-call | tf_op jit(solution)/shard_map/pallas_call | solution.py:158
  42.2 4.7 %shard_map.90 = (bf16[2,128,2048]{2,1,0:T(8,128)(2,1)}, bf16[2,128,2048]{2,1,0:T(8,128)(2,1)}) custom-call(s32[8]{0:T(128)} %stack.193.scalars, bf16[8,2,144,128]{3,2,1,0:T(8,128)(2,1)} %shard_map.87.weight_ref, bf16[1152,4096]{1,0:T(8,128)(2,1)} %own_ref.7, bf16[1152,4096]{1,0:T(8,128)(2,1)} %collective-permute-done.5.sib_ref), custom_call_target="tpu_custom_call" | custom-call | tf_op jit(solution)/shard_map/pallas_call | solution.py:158
  46.9 4.7 %shard_map.91 = (bf16[2,128,2048]{2,1,0:T(8,128)(2,1)}, bf16[2,128,2048]{2,1,0:T(8,128)(2,1)}) custom-call(s32[8]{0:T(128)} %stack.193.scalars, bf16[8,2,144,128]{3,2,1,0:T(8,128)(2,1)} %shard_map.87.weight_ref, bf16[1152,4096]{1,0:T(8,128)(2,1)} %own_ref.7, bf16[1152,4096]{1,0:T(8,128)(2,1)} %collective-permute-done.5.sib_ref), custom_call_target="tpu_custom_call" | custom-call | tf_op jit(solution)/shard_map/pallas_call | solution.py:158
  57.0 3.0 %collective-permute-start.13 = (bf16[2,288,768]{2,1,0:T(8,128)(2,1)S(1)}, bf16[2,288,768]{2,1,0:T(8,128)(2,1)}, u32[]{:S(2)}, u32[]{:S(2)}) collective-permute-start(bf16[2,288,768]{2,1,0:T(8,128)(2,1)S(1)} %bitcast.81), channel_id=1, source_target_pairs={{32,0},{48,16},{64,32},{80,48},{96,64},{112,80},{0,96},{16,112},{3... | collective-permute-start | bytes 2654216 | tf_op jit(solution)/shard_map/ppermute | solution.py:54
  64.9 12.1 %collective-permute-done.13.refs_6_ = bf16[2,288,768]{2,1,0:T(8,128)(2,1)} collective-permute-done((bf16[2,288,768]{2,1,0:T(8,128)(2,1)S(1)}, bf16[2,288,768]{2,1,0:T(8,128)(2,1)}, u32[]{:S(2)}, u32[]{:S(2)}) %collective-permute-start.13) | collective-permute-done | bytes 884768 | tf_op jit(solution)/shard_map/ppermute | solution.py:54
  77.0 3.4 %collective-permute-done.14.refs_10_ = bf16[2,288,768]{2,1,0:T(8,128)(2,1)S(1)} collective-permute-done((bf16[2,288,768]{2,1,0:T(8,128)(2,1)S(1)}, bf16[2,288,768]{2,1,0:T(8,128)(2,1)S(1)}, u32[]{:S(2)}, u32[]{:S(2)}) %collective-permute-start.14) | collective-permute-done | bytes 884768 | tf_op jit(solution)/shard_map/ppermute | solution.py:54
  83.7 3.0 %collective-permute-done.11.refs_1_ = bf16[8,144,512]{2,1,0:T(8,128)(2,1)S(1)} collective-permute-done((bf16[8,144,512]{2,1,0:T(8,128)(2,1)S(1)}, bf16[8,144,512]{2,1,0:T(8,128)(2,1)S(1)}, u32[]{:S(2)}, u32[]{:S(2)}) %collective-permute-start.11) | collective-permute-done | bytes 1179680 | tf_op jit(solution)/shard_map/ppermute | solution.py:50
  86.9 3.3 %collective-permute-start.17 = (bf16[4,144,512]{2,1,0:T(8,128)(2,1)S(1)}, bf16[4,144,512]{2,1,0:T(8,128)(2,1)S(1)}, u32[]{:S(2)}, u32[]{:S(2)}) collective-permute-start(bf16[4,144,512]{2,1,0:T(8,128)(2,1)S(1)} %slice.98), channel_id=1, source_target_pairs={{6,0},{7,1},{0,2},{1,3},{2,4},{3,5},{4,6},{5,7},{14,8},{15,9},{8,1... | collective-permute-start | bytes 1769480 | tf_op jit(solution)/shard_map/ppermute | solution.py:50
  91.7 8.3 %collective-permute-done.15 = bf16[4,144,512]{2,1,0:T(8,128)(2,1)S(1)} collective-permute-done((bf16[4,144,512]{2,1,0:T(8,128)(2,1)S(1)}, bf16[4,144,512]{2,1,0:T(8,128)(2,1)S(1)}, u32[]{:S(2)}, u32[]{:S(2)}) %collective-permute-start.15) | collective-permute-done | bytes 589856 | tf_op jit(solution)/shard_map/ppermute | solution.py:50
  100.2 3.1 %collective-permute-start.24 = (bf16[8,144,512]{2,1,0:T(8,128)(2,1)}, bf16[8,144,512]{2,1,0:T(8,128)(2,1)}, u32[]{:S(2)}, u32[]{:S(2)}) collective-permute-start(bf16[8,144,512]{2,1,0:T(8,128)(2,1)} %collective-permute-done.12.refs_0_), channel_id=1, source_target_pairs={{6,0},{7,1},{0,2},{1,3},{2,4},{3,5},{4,6},{5,7},{14,8},{15,9},{8,1... | collective-permute-start | bytes 3538952 | tf_op jit(solution)/shard_map/ppermute | solution.py:50
  108.2 11.8 %shard_map.92 = (bf16[8,4,72,512]{3,2,1,0:T(8,128)(2,1)}, bf16[8,4,72,512]{3,2,1,0:T(8,128)(2,1)}) custom-call(s32[2]{0:T(128)} %pad_add_fusion.scalars, bf16[288,288]{1,0:T(8,128)(2,1)} %fusion.7.order_ref, bf16[8,144,512]{2,1,0:T(8,128)(2,1)} %bitcast.80, bf16[8,144,512]{2,1,0:T(8,128)(2,1)} %copy-done.9, bf16[8,144,512]{2,1,0:T(8,128)(2,1)} %copy-done.11, ...), custom_call_target="tpu_custom_call" | custom-call | flops 14000000000 | bytes 15000000 | tf_op jit(solution)/shard_map/pallas_call | solution.py:203
  125.2 3.6 %collective-permute-done.23.refs_2_ = bf16[8,144,512]{2,1,0:T(8,128)(2,1)} collective-permute-done((bf16[8,144,512]{2,1,0:T(8,128)(2,1)S(1)}, bf16[8,144,512]{2,1,0:T(8,128)(2,1)}, u32[]{:S(2)}, u32[]{:S(2)}) %collective-permute-start.23) | collective-permute-done | bytes 1179680 | tf_op jit(solution)/shard_map/ppermute | solution.py:50
  128.9 11.8 %shard_map.93 = (bf16[8,4,72,512]{3,2,1,0:T(8,128)(2,1)}, bf16[8,4,72,512]{3,2,1,0:T(8,128)(2,1)}) custom-call(s32[2]{0:T(128)} %pad_add_fusion.scalars, bf16[288,288]{1,0:T(8,128)(2,1)} %fusion.7.order_ref, bf16[8,144,512]{2,1,0:T(8,128)(2,1)} %collective-permute-done.12.refs_0_, bf16[8,144,512]{2,1,0:T(8,128)(2,1)} %copy-done.15, ...), custom_call_target="tpu_custom_call" | custom-call | flops 14000000000 | bytes 15000000 | tf_op jit(solution)/shard_map/pallas_call | solution.py:203
  146.4 17.8 %collective-permute-done.30.refs_10_ = bf16[2,288,768]{2,1,0:T(8,128)(2,1)S(1)} collective-permute-done((bf16[2,288,768]{2,1,0:T(8,128)(2,1)}, bf16[2,288,768]{2,1,0:T(8,128)(2,1)S(1)}, u32[]{:S(2)}, u32[]{:S(2)}) %collective-permute-start.30) | collective-permute-done | bytes 884768 | tf_op jit(solution)/shard_map/ppermute | solution.py:54
  164.5 3.0 %collective-permute-start.31 = (bf16[2,288,768]{2,1,0:T(8,128)(2,1)S(1)}, bf16[2,288,768]{2,1,0:T(8,128)(2,1)S(1)}, u32[]{:S(2)}, u32[]{:S(2)}) collective-permute-start(bf16[2,288,768]{2,1,0:T(8,128)(2,1)S(1)} %collective-permute-done.26.refs_5_), channel_id=1, source_target_pairs={{32,0},{48,16},{64,32},{80,48},{96,64},{112,80},{0,96},{16,112},{3... | collective-permute-start | bytes 2654216 | tf_op jit(solution)/shard_map/ppermute | solution.py:54
  167.5 18.4 %collective-permute-done.31.refs_7_ = bf16[2,288,768]{2,1,0:T(8,128)(2,1)S(1)} collective-permute-done((bf16[2,288,768]{2,1,0:T(8,128)(2,1)S(1)}, bf16[2,288,768]{2,1,0:T(8,128)(2,1)S(1)}, u32[]{:S(2)}, u32[]{:S(2)}) %collective-permute-start.31) | collective-permute-done | bytes 884768 | tf_op jit(solution)/shard_map/ppermute | solution.py:54
  185.9 3.5 %collective-permute-done.32.refs_11_ = bf16[2,288,768]{2,1,0:T(8,128)(2,1)} collective-permute-done((bf16[2,288,768]{2,1,0:T(8,128)(2,1)S(1)}, bf16[2,288,768]{2,1,0:T(8,128)(2,1)}, u32[]{:S(2)}, u32[]{:S(2)}) %collective-permute-start.32) | collective-permute-done | bytes 884768 | tf_op jit(solution)/shard_map/ppermute | solution.py:54
  196.3 9.7 %shard_map.94.refs_12_ = f32[4,768,512]{2,1,0:T(8,128)} custom-call(bf16[8,4,72,512]{3,2,1,0:T(8,128)(2,1)} %get-tuple-element.67.refs_0_, bf16[8,4,72,512]{3,2,1,0:T(8,128)(2,1)} %copy-done.13, bf16[8,4,72,512]{3,2,1,0:T(8,128)(2,1)} %get-tuple-element.72.refs_2_, bf16[8,4,72,512]{3,2,1,0:T(8,128)(2,1)} %copy-done.14, bf16[2,288,768]{2,1,0:T(8,128)(2,1)} %bitcast.84, ...), custom_call_target="tpu_custom_call" | custom-call | flops 11000000512 | bytes 20000000 | tf_op jit(solution)/shard_map/pallas_call | solution.py:248
  206.3 10.5 %collective-permute-done.38 = bf16[2,128,2048]{2,1,0:T(8,128)(2,1)S(1)} collective-permute-done((bf16[2,128,2048]{2,1,0:T(8,128)(2,1)}, bf16[2,128,2048]{2,1,0:T(8,128)(2,1)S(1)}, u32[]{:S(2)}, u32[]{:S(2)}) %collective-permute-start.38) | collective-permute-done | bytes 1048608 | tf_op jit(solution)/shard_map/ppermute | solution.py:50
  221.5 10.9 %shard_map.95 = f32[4,768,512]{2,1,0:T(8,128)} custom-call(bf16[8,4,72,512]{3,2,1,0:T(8,128)(2,1)} %get-tuple-element.67.refs_0_, bf16[8,4,72,512]{3,2,1,0:T(8,128)(2,1)} %copy-done.13, bf16[8,4,72,512]{3,2,1,0:T(8,128)(2,1)} %get-tuple-element.72.refs_2_, bf16[8,4,72,512]{3,2,1,0:T(8,128)(2,1)} %copy-done.14, ...), custom_call_target="tpu_custom_call" | custom-call | flops 11000000512 | bytes 20000000 | tf_op jit(solution)/shard_map/pallas_call | solution.py:248
  (148 shorter events, 68.3 us)
Async XLA Ops:
  0.6 21.1 %collective-permute-start.5 = (bf16[1152,4096]{1,0:T(8,128)(2,1)}, bf16[1152,4096]{1,0:T(8,128)(2,1)}, u32[]{:S(2)}, u32[]{:S(2)}) collective-permute-start(bf16[1152,4096]{1,0:T(8,128)(2,1)} %own_ref.7), channel_id=1, source_target_pairs={{1,0},{0,1},{3,2},{2,3},{5,4},{4,5},{7,6},{6,7},{9,8},{8,9},{11,10... | collective-permute-start | bytes 28311560 | tf_op jit(solution)/shard_map/ppermute | solution.py:50
  8.5 21.3 %collective-permute-start = (bf16[4,144,512]{2,1,0:T(8,128)(2,1)}, bf16[4,144,512]{2,1,0:T(8,128)(2,1)}, u32[]{:S(2)}, u32[]{:S(2)}) collective-permute-start(bf16[4,144,512]{2,1,0:T(8,128)(2,1)} %get-tuple-element.45), channel_id=1, source_target_pairs={{16,0},{0,16},{48,32},{32,48},{80,64},{64,80},{112,96},{96,112},{1... | collective-permute-start | bytes 1769480 | tf_op jit(solution)/shard_map/ppermute | solution.py:54
  26.6 25.4 %collective-permute-start.10 = (bf16[2,128,2048]{2,1,0:T(8,128)(2,1)}, bf16[2,128,2048]{2,1,0:T(8,128)(2,1)}, u32[]{:S(2)}, u32[]{:S(2)}) collective-permute-start(bf16[2,128,2048]{2,1,0:T(8,128)(2,1)} %get-tuple-element.47), channel_id=1, source_target_pairs={{2,0},{3,1},{4,2},{5,3},{6,4},{7,5},{0,6},{1,7},{10,8},{11,9},{12,... | collective-permute-start | bytes 3145736 | tf_op jit(solution)/shard_map/ppermute | solution.py:50
  28.3 23.6 %collective-permute-start.9 = (bf16[2,128,2048]{2,1,0:T(8,128)(2,1)}, bf16[2,128,2048]{2,1,0:T(8,128)(2,1)S(1)}, u32[]{:S(2)}, u32[]{:S(2)}) collective-permute-start(bf16[2,128,2048]{2,1,0:T(8,128)(2,1)} %get-tuple-element.46), channel_id=1, source_target_pairs={{6,0},{7,1},{0,2},{1,3},{2,4},{3,5},{4,6},{5,7},{14,8},{15,9},{8,1... | collective-permute-start | bytes 3145736 | tf_op jit(solution)/shard_map/ppermute | solution.py:50
  53.2 29.2 %collective-permute-start.12 = (bf16[8,144,512]{2,1,0:T(8,128)(2,1)S(1)}, bf16[8,144,512]{2,1,0:T(8,128)(2,1)}, u32[]{:S(2)}, u32[]{:S(2)}) collective-permute-start(bf16[8,144,512]{2,1,0:T(8,128)(2,1)S(1)} %bitcast.77), channel_id=1, source_target_pairs={{8,0},{9,1},{10,2},{11,3},{12,4},{13,5},{14,6},{15,7},{0,8},{1,9},... | collective-permute-start | bytes 3538952 | tf_op jit(solution)/shard_map/ppermute | solution.py:50
  60.0 26.7 %collective-permute-start.11 = (bf16[8,144,512]{2,1,0:T(8,128)(2,1)S(1)}, bf16[8,144,512]{2,1,0:T(8,128)(2,1)S(1)}, u32[]{:S(2)}, u32[]{:S(2)}) collective-permute-start(bf16[8,144,512]{2,1,0:T(8,128)(2,1)S(1)} %bitcast.78), channel_id=1, source_target_pairs={{2,0},{3,1},{4,2},{5,3},{6,4},{7,5},{0,6},{1,7},{10,8},{11,9},{12,... | collective-permute-start | bytes 3538952 | tf_op jit(solution)/shard_map/ppermute | solution.py:50
  60.7 26.1 %collective-permute-start.16 = (bf16[8,144,512]{2,1,0:T(8,128)(2,1)S(1)}, bf16[8,144,512]{2,1,0:T(8,128)(2,1)S(1)}, u32[]{:S(2)}, u32[]{:S(2)}) collective-permute-start(bf16[8,144,512]{2,1,0:T(8,128)(2,1)S(1)} %bitcast.79), channel_id=1, source_target_pairs={{6,0},{7,1},{0,2},{1,3},{2,4},{3,5},{4,6},{5,7},{14,8},{15,9},{8,1... | collective-permute-start | bytes 3538952 | tf_op jit(solution)/shard_map/ppermute | solution.py:50
  80.4 23.0 %collective-permute-start.18 = (bf16[2,288,768]{2,1,0:T(8,128)(2,1)}, bf16[2,288,768]{2,1,0:T(8,128)(2,1)S(1)}, u32[]{:S(2)}, u32[]{:S(2)}) collective-permute-start(bf16[2,288,768]{2,1,0:T(8,128)(2,1)} %bitcast.55.refs_5_), channel_id=1, source_target_pairs={{32,0},{48,16},{64,32},{80,48},{96,64},{112,80},{0,96},{16,112},{3... | collective-permute-start | bytes 2654216 | tf_op jit(solution)/shard_map/ppermute | solution.py:54
  80.8 22.6 %collective-permute-start.19 = (bf16[2,288,768]{2,1,0:T(8,128)(2,1)}, bf16[2,288,768]{2,1,0:T(8,128)(2,1)}, u32[]{:S(2)}, u32[]{:S(2)}) collective-permute-start(bf16[2,288,768]{2,1,0:T(8,128)(2,1)} %bitcast.55.refs_5_), channel_id=1, source_target_pairs={{96,0},{112,16},{0,32},{16,48},{32,64},{48,80},{64,96},{80,112},{9... | collective-permute-start | bytes 2654216 | tf_op jit(solution)/shard_map/ppermute | solution.py:54
  82.4 23.9 %collective-permute-start.22 = (bf16[2,288,768]{2,1,0:T(8,128)(2,1)S(1)}, bf16[2,288,768]{2,1,0:T(8,128)(2,1)}, u32[]{:S(2)}, u32[]{:S(2)}) collective-permute-start(bf16[2,288,768]{2,1,0:T(8,128)(2,1)S(1)} %bitcast.83), channel_id=1, source_target_pairs={{16,0},{0,16},{48,32},{32,48},{80,64},{64,80},{112,96},{96,112},{1... | collective-permute-start | bytes 2654216 | tf_op jit(solution)/shard_map/ppermute | solution.py:54
  100.0 25.2 %collective-permute-start.21 = (bf16[8,144,512]{2,1,0:T(8,128)(2,1)}, bf16[8,144,512]{2,1,0:T(8,128)(2,1)S(1)}, u32[]{:S(2)}, u32[]{:S(2)}) collective-permute-start(bf16[8,144,512]{2,1,0:T(8,128)(2,1)} %collective-permute-done.12.refs_0_), channel_id=1, source_target_pairs={{2,0},{3,1},{4,2},{5,3},{6,4},{7,5},{0,6},{1,7},{10,8},{11,9},{12,... | collective-permute-start | bytes 3538952 | tf_op jit(solution)/shard_map/ppermute | solution.py:50
  100.2 25.0 %collective-permute-start.24 = (bf16[8,144,512]{2,1,0:T(8,128)(2,1)}, bf16[8,144,512]{2,1,0:T(8,128)(2,1)}, u32[]{:S(2)}, u32[]{:S(2)}) collective-permute-start(bf16[8,144,512]{2,1,0:T(8,128)(2,1)} %collective-permute-done.12.refs_0_), channel_id=1, source_target_pairs={{6,0},{7,1},{0,2},{1,3},{2,4},{3,5},{4,6},{5,7},{14,8},{15,9},{8,1... | collective-permute-start | bytes 3538952 | tf_op jit(solution)/shard_map/ppermute | solution.py:50
  106.3 22.6 %collective-permute-start.23 = (bf16[8,144,512]{2,1,0:T(8,128)(2,1)S(1)}, bf16[8,144,512]{2,1,0:T(8,128)(2,1)}, u32[]{:S(2)}, u32[]{:S(2)}) collective-permute-start(bf16[8,144,512]{2,1,0:T(8,128)(2,1)S(1)} %constant_dynamic-update-slice_fusion.refs_2_), channel_id=1, source_target_pairs={{8,0},{9,1},{10,2},{11,3},{12,4},{13,5},{14,6},{15,7},{0,8},{1,9},... | collective-permute-start | bytes 3538952 | tf_op jit(solution)/shard_map/ppermute | solution.py:50
  140.7 52.1 %collective-permute-start.25 = (bf16[8,4,72,512]{3,2,1,0:T(8,128)(2,1)}, bf16[8,4,72,512]{3,2,1,0:T(8,128)(2,1)S(1)}, u32[]{:S(2)}, u32[]{:S(2)}) collective-permute-start(bf16[8,4,72,512]{3,2,1,0:T(8,128)(2,1)} %get-tuple-element.73), channel_id=1, source_target_pairs={{1,0},{0,1},{3,2},{2,3},{5,4},{4,5},{7,6},{6,7},{9,8},{8,9},{11,10... | collective-permute-start | bytes 7077896 | tf_op jit(solution)/shard_map/ppermute | solution.py:50
  140.7 23.5 %collective-permute-start.30 = (bf16[2,288,768]{2,1,0:T(8,128)(2,1)}, bf16[2,288,768]{2,1,0:T(8,128)(2,1)S(1)}, u32[]{:S(2)}, u32[]{:S(2)}) collective-permute-start(bf16[2,288,768]{2,1,0:T(8,128)(2,1)} %collective-permute-done.22.refs_4_), channel_id=1, source_target_pairs={{96,0},{112,16},{0,32},{16,48},{32,64},{48,80},{64,96},{80,112},{9... | collective-permute-start | bytes 2654216 | tf_op jit(solution)/shard_map/ppermute | solution.py:54
  140.8 23.7 %collective-permute-start.26 = (bf16[2,288,768]{2,1,0:T(8,128)(2,1)}, bf16[2,288,768]{2,1,0:T(8,128)(2,1)S(1)}, u32[]{:S(2)}, u32[]{:S(2)}) collective-permute-start(bf16[2,288,768]{2,1,0:T(8,128)(2,1)} %bitcast.55.refs_5_), channel_id=1, source_target_pairs={{16,0},{0,16},{48,32},{32,48},{80,64},{64,80},{112,96},{96,112},{1... | collective-permute-start | bytes 2654216 | tf_op jit(solution)/shard_map/ppermute | solution.py:54
  143.1 48.3 %collective-permute-start.36 = (bf16[2,128,2048]{2,1,0:T(8,128)(2,1)}, bf16[2,128,2048]{2,1,0:T(8,128)(2,1)S(1)}, u32[]{:S(2)}, u32[]{:S(2)}) collective-permute-start(bf16[2,128,2048]{2,1,0:T(8,128)(2,1)} %get-tuple-element.82), channel_id=1, source_target_pairs={{2,0},{3,1},{4,2},{5,3},{6,4},{7,5},{0,6},{1,7},{10,8},{11,9},{12,... | collective-permute-start | bytes 3145736 | tf_op jit(solution)/shard_map/ppermute | solution.py:50
  144.9 46.6 %collective-permute-start.35 = (bf16[2,128,2048]{2,1,0:T(8,128)(2,1)S(1)}, bf16[2,128,2048]{2,1,0:T(8,128)(2,1)S(1)}, u32[]{:S(2)}, u32[]{:S(2)}) collective-permute-start(bf16[2,128,2048]{2,1,0:T(8,128)(2,1)S(1)} %add_convert_fusion.1), channel_id=1, source_target_pairs={{6,0},{7,1},{0,2},{1,3},{2,4},{3,5},{4,6},{5,7},{14,8},{15,9},{8,1... | collective-permute-start | bytes 3145736 | tf_op jit(solution)/shard_map/ppermute | solution.py:50
  164.5 21.4 %collective-permute-start.31 = (bf16[2,288,768]{2,1,0:T(8,128)(2,1)S(1)}, bf16[2,288,768]{2,1,0:T(8,128)(2,1)S(1)}, u32[]{:S(2)}, u32[]{:S(2)}) collective-permute-start(bf16[2,288,768]{2,1,0:T(8,128)(2,1)S(1)} %collective-permute-done.26.refs_5_), channel_id=1, source_target_pairs={{32,0},{48,16},{64,32},{80,48},{96,64},{112,80},{0,96},{16,112},{3... | collective-permute-start | bytes 2654216 | tf_op jit(solution)/shard_map/ppermute | solution.py:54
  167.5 21.9 %collective-permute-start.32 = (bf16[2,288,768]{2,1,0:T(8,128)(2,1)S(1)}, bf16[2,288,768]{2,1,0:T(8,128)(2,1)}, u32[]{:S(2)}, u32[]{:S(2)}) collective-permute-start(bf16[2,288,768]{2,1,0:T(8,128)(2,1)S(1)} %collective-permute-done.26.refs_5_), channel_id=1, source_target_pairs={{96,0},{112,16},{0,32},{16,48},{32,64},{48,80},{64,96},{80,112},{9... | collective-permute-start | bytes 2654216 | tf_op jit(solution)/shard_map/ppermute | solution.py:54
  189.4 32.1 %collective-permute-start.33 = (bf16[2,288,768]{2,1,0:T(8,128)(2,1)}, bf16[2,288,768]{2,1,0:T(8,128)(2,1)}, u32[]{:S(2)}, u32[]{:S(2)}) collective-permute-start(bf16[2,288,768]{2,1,0:T(8,128)(2,1)} %collective-permute-done.29.refs_6_), channel_id=1, source_target_pairs={{32,0},{48,16},{64,32},{80,48},{96,64},{112,80},{0,96},{16,112},{3... | collective-permute-start | bytes 2654216 | tf_op jit(solution)/shard_map/ppermute | solution.py:54
  189.8 31.6 %collective-permute-start.34 = (bf16[2,288,768]{2,1,0:T(8,128)(2,1)}, bf16[2,288,768]{2,1,0:T(8,128)(2,1)}, u32[]{:S(2)}, u32[]{:S(2)}) collective-permute-start(bf16[2,288,768]{2,1,0:T(8,128)(2,1)} %collective-permute-done.32.refs_11_), channel_id=1, source_target_pairs={{96,0},{112,16},{0,32},{16,48},{32,64},{48,80},{64,96},{80,112},{9... | collective-permute-start | bytes 2654216 | tf_op jit(solution)/shard_map/ppermute | solution.py:54
  194.2 22.6 %collective-permute-start.38 = (bf16[2,128,2048]{2,1,0:T(8,128)(2,1)}, bf16[2,128,2048]{2,1,0:T(8,128)(2,1)S(1)}, u32[]{:S(2)}, u32[]{:S(2)}) collective-permute-start(bf16[2,128,2048]{2,1,0:T(8,128)(2,1)} %get-tuple-element.83), channel_id=1, source_target_pairs={{6,0},{7,1},{0,2},{1,3},{2,4},{3,5},{4,6},{5,7},{14,8},{15,9},{8,1... | collective-permute-start | bytes 3145736 | tf_op jit(solution)/shard_map/ppermute | solution.py:50
  195.7 23.4 %collective-permute-start.39 = (bf16[2,128,2048]{2,1,0:T(8,128)(2,1)S(1)}, bf16[2,128,2048]{2,1,0:T(8,128)(2,1)}, u32[]{:S(2)}, u32[]{:S(2)}) collective-permute-start(bf16[2,128,2048]{2,1,0:T(8,128)(2,1)S(1)} %add_convert_fusion), channel_id=1, source_target_pairs={{2,0},{3,1},{4,2},{5,3},{6,4},{7,5},{0,6},{1,7},{10,8},{11,9},{12,... | collective-permute-start | bytes 3145736 | tf_op jit(solution)/shard_map/ppermute | solution.py:50
  (39 other events, 568.0 us)

commit v3 on v2

--- a/solution.py
+++ b/solution.py
@@ -24,6 +24,7 @@
 LONG = TOK + 16
 QUAD = 4
 BATCH = 4
+STEP = 2
 
 VMEM = 56 * 1024 * 1024
 
@@ -176,11 +177,16 @@
 
 def sent_kernel(scalars, order_ref, *refs):
     tok_refs, out_refs = refs[:QUAD], refs[QUAD:]
-    tokens = jnp.concatenate([ref[0, :TOK, :] for ref in tok_refs], axis=0)
+    for g in range(STEP):
+        sent_rows(scalars, order_ref, [ref.at[g] for ref in tok_refs], [ref.at[g] for ref in out_refs])
+
+
+def sent_rows(scalars, order_ref, tok_refs, out_refs):
+    tokens = jnp.concatenate([ref[:TOK, :] for ref in tok_refs], axis=0)
     blocks = []
     for j in range(2):
         for ref in tok_refs:
-            table = ref[0, TOK:, :TOK].astype(jnp.float32)
+            table = ref[TOK:, :TOK].astype(jnp.float32)
             blocks.append(([table[k : k + 1, :] for k in range(2 * TOP)], scalars[j]))
     gates = slot_weights(blocks)
     none = jnp.zeros((SLOT, TOK), jnp.float32)
@@ -195,7 +201,7 @@
         route = jnp.dot(order_ref[...], route, preferred_element_type=jnp.float32)
         sent = jnp.dot(route.astype(jnp.bfloat16), tokens, preferred_element_type=jnp.float32)
         for e in range(E):
-            out_ref[0, e] = sent[e * SLOT : (e + 1) * SLOT, :].astype(jnp.bfloat16)
+            out_ref[e] = sent[e * SLOT : (e + 1) * SLOT, :].astype(jnp.bfloat16)
 
 
 def build_sent(scalars, order, tokens):
@@ -204,10 +210,10 @@
         sent_kernel,
         grid_spec=pltpu.PrefetchScalarGridSpec(
             num_scalar_prefetch=1,
-            grid=(NDP,),
+            grid=(NDP // STEP,),
             in_specs=[pl.BlockSpec((QUAD * SLOT, QUAD * SLOT), lambda g, s: (0, 0))]
-            + [pl.BlockSpec((1, LONG, COLS), lambda g, s: (g, 0, 0)) for _ in range(QUAD)],
-            out_specs=[pl.BlockSpec((1,) + rows[1:], lambda g, s: (g, 0, 0, 0))] * 2,
+            + [pl.BlockSpec((STEP, LONG, COLS), lambda g, s: (g, 0, 0)) for _ in range(QUAD)],
+            out_specs=[pl.BlockSpec((STEP,) + rows[1:], lambda g, s: (g, 0, 0, 0))] * 2,
         ),
         out_shape=[jax.ShapeDtypeStruct(rows, jnp.bfloat16)] * 2,
         compiler_params=pltpu.CompilerParams(vmem_limit_bytes=VMEM),

time: 236 us -> 235 us (level)
  no operation moved by 1% of the time
where the time goes in v3:
time: 235 us; the launch traced here: 234 us
  waiting for transfers between devices  90.1 us (38%)
  Pallas kernels  67.2 us (29%)
  starting transfers between devices  51.1 us (22%)
  other arithmetic  13.9 us (6%)
  local copies, waits for them, and re-layouts  8.17 us (3%)
  matrix products  2.6 us (1%)
    ppermute x18, waiting for transfers between devices, dp_from(): return lax.ppermute(value, 'dp', dp_perm(dy, dzh))  61.1 us
    ppermute x23, waiting for transfers between devices, ex_from(): return lax.ppermute(value, 'expert', ex_perm(dzl, dx, dc))  29.1 us
    ppermute x23, starting transfers between devices, ex_from(): return lax.ppermute(value, 'expert', ex_perm(dzl, dx, dc))  27 us
    ppermute x18, starting transfers between devices, dp_from(): return lax.ppermute(value, 'dp', dp_perm(dy, dzh))  24.1 us
    pallas_call x2, Pallas kernels, build_sent(): pl.pallas_call(sent_kernel, grid_spec=pltpu.PrefetchScalarGridSpec(num_sc...  22.1 us
    pallas_call x2, Pallas kernels, weight_grad(): pl.pallas_call(functools.partial(weight_kernel, counts=tuple((len(s) for...  20.6 us
    pallas_call x4, Pallas kernels, combine(): pl.pallas_call(functools.partial(combine_kernel, outs=outs), grid_spec=pl...  18.8 us
    convert_element_type x6, other arithmetic, add(): return sum((v.astype(jnp.float32) for v in values)).astype(jnp.bfloat16)  5.35 us
  transfers between devices with their start and end apart: 41, of which 17 were waited for; matrix products, arithmetic and copies ran while one was open for 7% of the time, Pallas kernels for 29%

profile of v3, /device:TPU:6, one launch (start us, length us, event | category | flops | bytes accessed | tf_op | source)
XLA Modules:
  0.0 234.2 jit_solution(2589544725086832398)
XLA Ops:
  5.5 3.0 %shard_map.86 = (bf16[4,144,512]{2,1,0:T(8,128)(2,1)}, bf16[4,144,512]{2,1,0:T(8,128)(2,1)}) custom-call(s32[8]{0:T(128)} %stack.181.targets, bf16[128,4096]{1,0:T(8,128)(2,1)} %grad_ref.1, f32[32,128]{1,0:T(8,128)} %copy-done.12), custom_call_target="tpu_custom_call" | custom-call | tf_op jit(solution)/shard_map/pallas_call | solution.py:97
  8.5 3.6 %collective-permute-start = (bf16[4,144,512]{2,1,0:T(8,128)(2,1)}, bf16[4,144,512]{2,1,0:T(8,128)(2,1)}, u32[]{:S(2)}, u32[]{:S(2)}) collective-permute-start(bf16[4,144,512]{2,1,0:T(8,128)(2,1)} %get-tuple-element.45), channel_id=1, source_target_pairs={{16,0},{0,16},{48,32},{32,48},{80,64},{64,80},{112,96},{96,112},{1... | collective-permute-start | bytes 1769480 | tf_op jit(solution)/shard_map/ppermute | solution.py:55
  21.8 4.8 %shard_map.88 = (bf16[2,128,2048]{2,1,0:T(8,128)(2,1)}, bf16[2,128,2048]{2,1,0:T(8,128)(2,1)}) custom-call(s32[8]{0:T(128)} %stack.193.scalars, bf16[8,2,144,128]{3,2,1,0:T(8,128)(2,1)} %shard_map.87.weight_ref, bf16[1152,4096]{1,0:T(8,128)(2,1)} %own_ref.7, bf16[1152,4096]{1,0:T(8,128)(2,1)} %collective-permute-done.5.sib_ref), custom_call_target="tpu_custom_call" | custom-call | tf_op jit(solution)/shard_map/pallas_call | solution.py:159
  31.9 3.0 %collective-permute-start.6 = (bf16[2,144,512]{2,1,0:T(8,128)(2,1)}, bf16[2,144,512]{2,1,0:T(8,128)(2,1)S(1)}, u32[]{:S(2)}, u32[]{:S(2)}) collective-permute-start(bf16[2,144,512]{2,1,0:T(8,128)(2,1)} %get-tuple-element.89), channel_id=1, source_target_pairs={{32,0},{48,16},{64,32},{80,48},{96,64},{112,80},{0,96},{16,112},{3... | collective-permute-start | bytes 884744 | tf_op jit(solution)/shard_map/ppermute | solution.py:55
  37.5 4.7 %shard_map.89 = (bf16[2,128,2048]{2,1,0:T(8,128)(2,1)}, bf16[2,128,2048]{2,1,0:T(8,128)(2,1)}) custom-call(s32[8]{0:T(128)} %stack.193.scalars, bf16[8,2,144,128]{3,2,1,0:T(8,128)(2,1)} %shard_map.87.weight_ref, bf16[1152,4096]{1,0:T(8,128)(2,1)} %own_ref.7, bf16[1152,4096]{1,0:T(8,128)(2,1)} %collective-permute-done.5.sib_ref), custom_call_target="tpu_custom_call" | custom-call | tf_op jit(solution)/shard_map/pallas_call | solution.py:159
  42.2 4.7 %shard_map.90 = (bf16[2,128,2048]{2,1,0:T(8,128)(2,1)}, bf16[2,128,2048]{2,1,0:T(8,128)(2,1)}) custom-call(s32[8]{0:T(128)} %stack.193.scalars, bf16[8,2,144,128]{3,2,1,0:T(8,128)(2,1)} %shard_map.87.weight_ref, bf16[1152,4096]{1,0:T(8,128)(2,1)} %own_ref.7, bf16[1152,4096]{1,0:T(8,128)(2,1)} %collective-permute-done.5.sib_ref), custom_call_target="tpu_custom_call" | custom-call | tf_op jit(solution)/shard_map/pallas_call | solution.py:159
  46.9 4.7 %shard_map.91 = (bf16[2,128,2048]{2,1,0:T(8,128)(2,1)}, bf16[2,128,2048]{2,1,0:T(8,128)(2,1)}) custom-call(s32[8]{0:T(128)} %stack.193.scalars, bf16[8,2,144,128]{3,2,1,0:T(8,128)(2,1)} %shard_map.87.weight_ref, bf16[1152,4096]{1,0:T(8,128)(2,1)} %own_ref.7, bf16[1152,4096]{1,0:T(8,128)(2,1)} %collective-permute-done.5.sib_ref), custom_call_target="tpu_custom_call" | custom-call | tf_op jit(solution)/shard_map/pallas_call | solution.py:159
  57.0 3.0 %collective-permute-start.13 = (bf16[2,288,768]{2,1,0:T(8,128)(2,1)S(1)}, bf16[2,288,768]{2,1,0:T(8,128)(2,1)}, u32[]{:S(2)}, u32[]{:S(2)}) collective-permute-start(bf16[2,288,768]{2,1,0:T(8,128)(2,1)S(1)} %bitcast.81), channel_id=1, source_target_pairs={{32,0},{48,16},{64,32},{80,48},{96,64},{112,80},{0,96},{16,112},{3... | collective-permute-start | bytes 2654216 | tf_op jit(solution)/shard_map/ppermute | solution.py:55
  64.9 12.1 %collective-permute-done.13.refs_6_ = bf16[2,288,768]{2,1,0:T(8,128)(2,1)} collective-permute-done((bf16[2,288,768]{2,1,0:T(8,128)(2,1)S(1)}, bf16[2,288,768]{2,1,0:T(8,128)(2,1)}, u32[]{:S(2)}, u32[]{:S(2)}) %collective-permute-start.13) | collective-permute-done | bytes 884768 | tf_op jit(solution)/shard_map/ppermute | solution.py:55
  77.0 3.4 %collective-permute-done.14.refs_10_ = bf16[2,288,768]{2,1,0:T(8,128)(2,1)S(1)} collective-permute-done((bf16[2,288,768]{2,1,0:T(8,128)(2,1)S(1)}, bf16[2,288,768]{2,1,0:T(8,128)(2,1)S(1)}, u32[]{:S(2)}, u32[]{:S(2)}) %collective-permute-start.14) | collective-permute-done | bytes 884768 | tf_op jit(solution)/shard_map/ppermute | solution.py:55
  83.7 3.0 %collective-permute-done.11.refs_1_ = bf16[8,144,512]{2,1,0:T(8,128)(2,1)S(1)} collective-permute-done((bf16[8,144,512]{2,1,0:T(8,128)(2,1)S(1)}, bf16[8,144,512]{2,1,0:T(8,128)(2,1)S(1)}, u32[]{:S(2)}, u32[]{:S(2)}) %collective-permute-start.11) | collective-permute-done | bytes 1179680 | tf_op jit(solution)/shard_map/ppermute | solution.py:51
  86.9 3.3 %collective-permute-start.17 = (bf16[4,144,512]{2,1,0:T(8,128)(2,1)S(1)}, bf16[4,144,512]{2,1,0:T(8,128)(2,1)S(1)}, u32[]{:S(2)}, u32[]{:S(2)}) collective-permute-start(bf16[4,144,512]{2,1,0:T(8,128)(2,1)S(1)} %slice.98), channel_id=1, source_target_pairs={{6,0},{7,1},{0,2},{1,3},{2,4},{3,5},{4,6},{5,7},{14,8},{15,9},{8,1... | collective-permute-start | bytes 1769480 | tf_op jit(solution)/shard_map/ppermute | solution.py:51
  91.7 8.3 %collective-permute-done.15 = bf16[4,144,512]{2,1,0:T(8,128)(2,1)S(1)} collective-permute-done((bf16[4,144,512]{2,1,0:T(8,128)(2,1)S(1)}, bf16[4,144,512]{2,1,0:T(8,128)(2,1)S(1)}, u32[]{:S(2)}, u32[]{:S(2)}) %collective-permute-start.15) | collective-permute-done | bytes 589856 | tf_op jit(solution)/shard_map/ppermute | solution.py:51
  100.2 3.1 %collective-permute-start.24 = (bf16[8,144,512]{2,1,0:T(8,128)(2,1)}, bf16[8,144,512]{2,1,0:T(8,128)(2,1)}, u32[]{:S(2)}, u32[]{:S(2)}) collective-permute-start(bf16[8,144,512]{2,1,0:T(8,128)(2,1)} %collective-permute-done.12.refs_0_), channel_id=1, source_target_pairs={{6,0},{7,1},{0,2},{1,3},{2,4},{3,5},{4,6},{5,7},{14,8},{15,9},{8,1... | collective-permute-start | bytes 3538952 | tf_op jit(solution)/shard_map/ppermute | solution.py:51
  108.2 11.0 %shard_map.92 = (bf16[8,4,72,512]{3,2,1,0:T(8,128)(2,1)}, bf16[8,4,72,512]{3,2,1,0:T(8,128)(2,1)}) custom-call(s32[2]{0:T(128)} %pad_add_fusion.scalars, bf16[288,288]{1,0:T(8,128)(2,1)} %fusion.7.order_ref, bf16[8,144,512]{2,1,0:T(8,128)(2,1)} %bitcast.80, bf16[8,144,512]{2,1,0:T(8,128)(2,1)} %copy-done.9, bf16[8,144,512]{2,1,0:T(8,128)(2,1)} %copy-done.11, ...), custom_call_target="tpu_custom_call" | custom-call | flops 14000000000 | bytes 15000000 | tf_op jit(solution)/shard_map/pallas_call | solution.py:209
  125.2 3.6 %collective-permute-done.23.refs_2_ = bf16[8,144,512]{2,1,0:T(8,128)(2,1)} collective-permute-done((bf16[8,144,512]{2,1,0:T(8,128)(2,1)S(1)}, bf16[8,144,512]{2,1,0:T(8,128)(2,1)}, u32[]{:S(2)}, u32[]{:S(2)}) %collective-permute-start.23) | collective-permute-done | bytes 1179680 | tf_op jit(solution)/shard_map/ppermute | solution.py:51
  128.9 11.0 %shard_map.93 = (bf16[8,4,72,512]{3,2,1,0:T(8,128)(2,1)}, bf16[8,4,72,512]{3,2,1,0:T(8,128)(2,1)}) custom-call(s32[2]{0:T(128)} %pad_add_fusion.scalars, bf16[288,288]{1,0:T(8,128)(2,1)} %fusion.7.order_ref, bf16[8,144,512]{2,1,0:T(8,128)(2,1)} %collective-permute-done.12.refs_0_, bf16[8,144,512]{2,1,0:T(8,128)(2,1)} %copy-done.15, ...), custom_call_target="tpu_custom_call" | custom-call | flops 14000000000 | bytes 15000000 | tf_op jit(solution)/shard_map/pallas_call | solution.py:209
  146.4 17.0 %collective-permute-done.30.refs_10_ = bf16[2,288,768]{2,1,0:T(8,128)(2,1)S(1)} collective-permute-done((bf16[2,288,768]{2,1,0:T(8,128)(2,1)}, bf16[2,288,768]{2,1,0:T(8,128)(2,1)S(1)}, u32[]{:S(2)}, u32[]{:S(2)}) %collective-permute-start.30) | collective-permute-done | bytes 884768 | tf_op jit(solution)/shard_map/ppermute | solution.py:55
  163.7 3.0 %collective-permute-start.31 = (bf16[2,288,768]{2,1,0:T(8,128)(2,1)S(1)}, bf16[2,288,768]{2,1,0:T(8,128)(2,1)S(1)}, u32[]{:S(2)}, u32[]{:S(2)}) collective-permute-start(bf16[2,288,768]{2,1,0:T(8,128)(2,1)S(1)} %collective-permute-done.26.refs_5_), channel_id=1, source_target_pairs={{32,0},{48,16},{64,32},{80,48},{96,64},{112,80},{0,96},{16,112},{3... | collective-permute-start | bytes 2654216 | tf_op jit(solution)/shard_map/ppermute | solution.py:55
  166.7 18.4 %collective-permute-done.31.refs_7_ = bf16[2,288,768]{2,1,0:T(8,128)(2,1)S(1)} collective-permute-done((bf16[2,288,768]{2,1,0:T(8,128)(2,1)S(1)}, bf16[2,288,768]{2,1,0:T(8,128)(2,1)S(1)}, u32[]{:S(2)}, u32[]{:S(2)}) %collective-permute-start.31) | collective-permute-done | bytes 884768 | tf_op jit(solution)/shard_map/ppermute | solution.py:55
  185.1 3.5 %collective-permute-done.32.refs_11_ = bf16[2,288,768]{2,1,0:T(8,128)(2,1)} collective-permute-done((bf16[2,288,768]{2,1,0:T(8,128)(2,1)S(1)}, bf16[2,288,768]{2,1,0:T(8,128)(2,1)}, u32[]{:S(2)}, u32[]{:S(2)}) %collective-permute-start.32) | collective-permute-done | bytes 884768 | tf_op jit(solution)/shard_map/ppermute | solution.py:55
  195.5 9.7 %shard_map.94.refs_12_ = f32[4,768,512]{2,1,0:T(8,128)} custom-call(bf16[8,4,72,512]{3,2,1,0:T(8,128)(2,1)} %get-tuple-element.67.refs_0_, bf16[8,4,72,512]{3,2,1,0:T(8,128)(2,1)} %copy-done.13, bf16[8,4,72,512]{3,2,1,0:T(8,128)(2,1)} %get-tuple-element.72.refs_2_, bf16[8,4,72,512]{3,2,1,0:T(8,128)(2,1)} %copy-done.14, bf16[2,288,768]{2,1,0:T(8,128)(2,1)} %bitcast.84, ...), custom_call_target="tpu_custom_call" | custom-call | flops 11000000512 | bytes 20000000 | tf_op jit(solution)/shard_map/pallas_call | solution.py:254
  205.5 10.5 %collective-permute-done.38 = bf16[2,128,2048]{2,1,0:T(8,128)(2,1)S(1)} collective-permute-done((bf16[2,128,2048]{2,1,0:T(8,128)(2,1)}, bf16[2,128,2048]{2,1,0:T(8,128)(2,1)S(1)}, u32[]{:S(2)}, u32[]{:S(2)}) %collective-permute-start.38) | collective-permute-done | bytes 1048608 | tf_op jit(solution)/shard_map/ppermute | solution.py:51
  220.7 10.9 %shard_map.95 = f32[4,768,512]{2,1,0:T(8,128)} custom-call(bf16[8,4,72,512]{3,2,1,0:T(8,128)(2,1)} %get-tuple-element.67.refs_0_, bf16[8,4,72,512]{3,2,1,0:T(8,128)(2,1)} %copy-done.13, bf16[8,4,72,512]{3,2,1,0:T(8,128)(2,1)} %get-tuple-element.72.refs_2_, bf16[8,4,72,512]{3,2,1,0:T(8,128)(2,1)} %copy-done.14, ...), custom_call_target="tpu_custom_call" | custom-call | flops 11000000512 | bytes 20000000 | tf_op jit(solution)/shard_map/pallas_call | solution.py:254
  (148 shorter events, 69.9 us)
Async XLA Ops:
  0.6 21.1 %collective-permute-start.5 = (bf16[1152,4096]{1,0:T(8,128)(2,1)}, bf16[1152,4096]{1,0:T(8,128)(2,1)}, u32[]{:S(2)}, u32[]{:S(2)}) collective-permute-start(bf16[1152,4096]{1,0:T(8,128)(2,1)} %own_ref.7), channel_id=1, source_target_pairs={{1,0},{0,1},{3,2},{2,3},{5,4},{4,5},{7,6},{6,7},{9,8},{8,9},{11,10... | collective-permute-start | bytes 28311560 | tf_op jit(solution)/shard_map/ppermute | solution.py:51
  8.5 21.3 %collective-permute-start = (bf16[4,144,512]{2,1,0:T(8,128)(2,1)}, bf16[4,144,512]{2,1,0:T(8,128)(2,1)}, u32[]{:S(2)}, u32[]{:S(2)}) collective-permute-start(bf16[4,144,512]{2,1,0:T(8,128)(2,1)} %get-tuple-element.45), channel_id=1, source_target_pairs={{16,0},{0,16},{48,32},{32,48},{80,64},{64,80},{112,96},{96,112},{1... | collective-permute-start | bytes 1769480 | tf_op jit(solution)/shard_map/ppermute | solution.py:55
  26.6 25.4 %collective-permute-start.10 = (bf16[2,128,2048]{2,1,0:T(8,128)(2,1)}, bf16[2,128,2048]{2,1,0:T(8,128)(2,1)}, u32[]{:S(2)}, u32[]{:S(2)}) collective-permute-start(bf16[2,128,2048]{2,1,0:T(8,128)(2,1)} %get-tuple-element.47), channel_id=1, source_target_pairs={{2,0},{3,1},{4,2},{5,3},{6,4},{7,5},{0,6},{1,7},{10,8},{11,9},{12,... | collective-permute-start | bytes 3145736 | tf_op jit(solution)/shard_map/ppermute | solution.py:51
  28.3 23.6 %collective-permute-start.9 = (bf16[2,128,2048]{2,1,0:T(8,128)(2,1)}, bf16[2,128,2048]{2,1,0:T(8,128)(2,1)S(1)}, u32[]{:S(2)}, u32[]{:S(2)}) collective-permute-start(bf16[2,128,2048]{2,1,0:T(8,128)(2,1)} %get-tuple-element.46), channel_id=1, source_target_pairs={{6,0},{7,1},{0,2},{1,3},{2,4},{3,5},{4,6},{5,7},{14,8},{15,9},{8,1... | collective-permute-start | bytes 3145736 | tf_op jit(solution)/shard_map/ppermute | solution.py:51
  53.2 29.2 %collective-permute-start.12 = (bf16[8,144,512]{2,1,0:T(8,128)(2,1)S(1)}, bf16[8,144,512]{2,1,0:T(8,128)(2,1)}, u32[]{:S(2)}, u32[]{:S(2)}) collective-permute-start(bf16[8,144,512]{2,1,0:T(8,128)(2,1)S(1)} %bitcast.77), channel_id=1, source_target_pairs={{8,0},{9,1},{10,2},{11,3},{12,4},{13,5},{14,6},{15,7},{0,8},{1,9},... | collective-permute-start | bytes 3538952 | tf_op jit(solution)/shard_map/ppermute | solution.py:51
  60.0 26.7 %collective-permute-start.11 = (bf16[8,144,512]{2,1,0:T(8,128)(2,1)S(1)}, bf16[8,144,512]{2,1,0:T(8,128)(2,1)S(1)}, u32[]{:S(2)}, u32[]{:S(2)}) collective-permute-start(bf16[8,144,512]{2,1,0:T(8,128)(2,1)S(1)} %bitcast.78), channel_id=1, source_target_pairs={{2,0},{3,1},{4,2},{5,3},{6,4},{7,5},{0,6},{1,7},{10,8},{11,9},{12,... | collective-permute-start | bytes 3538952 | tf_op jit(solution)/shard_map/ppermute | solution.py:51
  60.7 26.1 %collective-permute-start.16 = (bf16[8,144,512]{2,1,0:T(8,128)(2,1)S(1)}, bf16[8,144,512]{2,1,0:T(8,128)(2,1)S(1)}, u32[]{:S(2)}, u32[]{:S(2)}) collective-permute-start(bf16[8,144,512]{2,1,0:T(8,128)(2,1)S(1)} %bitcast.79), channel_id=1, source_target_pairs={{6,0},{7,1},{0,2},{1,3},{2,4},{3,5},{4,6},{5,7},{14,8},{15,9},{8,1... | collective-permute-start | bytes 3538952 | tf_op jit(solution)/shard_map/ppermute | solution.py:51
  80.4 23.0 %collective-permute-start.18 = (bf16[2,288,768]{2,1,0:T(8,128)(2,1)}, bf16[2,288,768]{2,1,0:T(8,128)(2,1)S(1)}, u32[]{:S(2)}, u32[]{:S(2)}) collective-permute-start(bf16[2,288,768]{2,1,0:T(8,128)(2,1)} %bitcast.55.refs_5_), channel_id=1, source_target_pairs={{32,0},{48,16},{64,32},{80,48},{96,64},{112,80},{0,96},{16,112},{3... | collective-permute-start | bytes 2654216 | tf_op jit(solution)/shard_map/ppermute | solution.py:55
  80.8 22.6 %collective-permute-start.19 = (bf16[2,288,768]{2,1,0:T(8,128)(2,1)}, bf16[2,288,768]{2,1,0:T(8,128)(2,1)}, u32[]{:S(2)}, u32[]{:S(2)}) collective-permute-start(bf16[2,288,768]{2,1,0:T(8,128)(2,1)} %bitcast.55.refs_5_), channel_id=1, source_target_pairs={{96,0},{112,16},{0,32},{16,48},{32,64},{48,80},{64,96},{80,112},{9... | collective-permute-start | bytes 2654216 | tf_op jit(solution)/shard_map/ppermute | solution.py:55
  82.4 23.9 %collective-permute-start.22 = (bf16[2,288,768]{2,1,0:T(8,128)(2,1)S(1)}, bf16[2,288,768]{2,1,0:T(8,128)(2,1)}, u32[]{:S(2)}, u32[]{:S(2)}) collective-permute-start(bf16[2,288,768]{2,1,0:T(8,128)(2,1)S(1)} %bitcast.83), channel_id=1, source_target_pairs={{16,0},{0,16},{48,32},{32,48},{80,64},{64,80},{112,96},{96,112},{1... | collective-permute-start | bytes 2654216 | tf_op jit(solution)/shard_map/ppermute | solution.py:55
  100.0 25.2 %collective-permute-start.21 = (bf16[8,144,512]{2,1,0:T(8,128)(2,1)}, bf16[8,144,512]{2,1,0:T(8,128)(2,1)S(1)}, u32[]{:S(2)}, u32[]{:S(2)}) collective-permute-start(bf16[8,144,512]{2,1,0:T(8,128)(2,1)} %collective-permute-done.12.refs_0_), channel_id=1, source_target_pairs={{2,0},{3,1},{4,2},{5,3},{6,4},{7,5},{0,6},{1,7},{10,8},{11,9},{12,... | collective-permute-start | bytes 3538952 | tf_op jit(solution)/shard_map/ppermute | solution.py:51
  100.2 25.0 %collective-permute-start.24 = (bf16[8,144,512]{2,1,0:T(8,128)(2,1)}, bf16[8,144,512]{2,1,0:T(8,128)(2,1)}, u32[]{:S(2)}, u32[]{:S(2)}) collective-permute-start(bf16[8,144,512]{2,1,0:T(8,128)(2,1)} %collective-permute-done.12.refs_0_), channel_id=1, source_target_pairs={{6,0},{7,1},{0,2},{1,3},{2,4},{3,5},{4,6},{5,7},{14,8},{15,9},{8,1... | collective-permute-start | bytes 3538952 | tf_op jit(solution)/shard_map/ppermute | solution.py:51
  106.3 22.6 %collective-permute-start.23 = (bf16[8,144,512]{2,1,0:T(8,128)(2,1)S(1)}, bf16[8,144,512]{2,1,0:T(8,128)(2,1)}, u32[]{:S(2)}, u32[]{:S(2)}) collective-permute-start(bf16[8,144,512]{2,1,0:T(8,128)(2,1)S(1)} %constant_dynamic-update-slice_fusion.refs_2_), channel_id=1, source_target_pairs={{8,0},{9,1},{10,2},{11,3},{12,4},{13,5},{14,6},{15,7},{0,8},{1,9},... | collective-permute-start | bytes 3538952 | tf_op jit(solution)/shard_map/ppermute | solution.py:51
  139.9 52.1 %collective-permute-start.25 = (bf16[8,4,72,512]{3,2,1,0:T(8,128)(2,1)}, bf16[8,4,72,512]{3,2,1,0:T(8,128)(2,1)S(1)}, u32[]{:S(2)}, u32[]{:S(2)}) collective-permute-start(bf16[8,4,72,512]{3,2,1,0:T(8,128)(2,1)} %get-tuple-element.73), channel_id=1, source_target_pairs={{1,0},{0,1},{3,2},{2,3},{5,4},{4,5},{7,6},{6,7},{9,8},{8,9},{11,10... | collective-permute-start | bytes 7077896 | tf_op jit(solution)/shard_map/ppermute | solution.py:51
  139.9 23.5 %collective-permute-start.30 = (bf16[2,288,768]{2,1,0:T(8,128)(2,1)}, bf16[2,288,768]{2,1,0:T(8,128)(2,1)S(1)}, u32[]{:S(2)}, u32[]{:S(2)}) collective-permute-start(bf16[2,288,768]{2,1,0:T(8,128)(2,1)} %collective-permute-done.22.refs_4_), channel_id=1, source_target_pairs={{96,0},{112,16},{0,32},{16,48},{32,64},{48,80},{64,96},{80,112},{9... | collective-permute-start | bytes 2654216 | tf_op jit(solution)/shard_map/ppermute | solution.py:55
  140.0 23.7 %collective-permute-start.26 = (bf16[2,288,768]{2,1,0:T(8,128)(2,1)}, bf16[2,288,768]{2,1,0:T(8,128)(2,1)S(1)}, u32[]{:S(2)}, u32[]{:S(2)}) collective-permute-start(bf16[2,288,768]{2,1,0:T(8,128)(2,1)} %bitcast.55.refs_5_), channel_id=1, source_target_pairs={{16,0},{0,16},{48,32},{32,48},{80,64},{64,80},{112,96},{96,112},{1... | collective-permute-start | bytes 2654216 | tf_op jit(solution)/shard_map/ppermute | solution.py:55
  142.3 48.3 %collective-permute-start.36 = (bf16[2,128,2048]{2,1,0:T(8,128)(2,1)}, bf16[2,128,2048]{2,1,0:T(8,128)(2,1)S(1)}, u32[]{:S(2)}, u32[]{:S(2)}) collective-permute-start(bf16[2,128,2048]{2,1,0:T(8,128)(2,1)} %get-tuple-element.82), channel_id=1, source_target_pairs={{2,0},{3,1},{4,2},{5,3},{6,4},{7,5},{0,6},{1,7},{10,8},{11,9},{12,... | collective-permute-start | bytes 3145736 | tf_op jit(solution)/shard_map/ppermute | solution.py:51
  144.9 45.8 %collective-permute-start.35 = (bf16[2,128,2048]{2,1,0:T(8,128)(2,1)S(1)}, bf16[2,128,2048]{2,1,0:T(8,128)(2,1)S(1)}, u32[]{:S(2)}, u32[]{:S(2)}) collective-permute-start(bf16[2,128,2048]{2,1,0:T(8,128)(2,1)S(1)} %add_convert_fusion.1), channel_id=1, source_target_pairs={{6,0},{7,1},{0,2},{1,3},{2,4},{3,5},{4,6},{5,7},{14,8},{15,9},{8,1... | collective-permute-start | bytes 3145736 | tf_op jit(solution)/shard_map/ppermute | solution.py:51
  163.7 21.4 %collective-permute-start.31 = (bf16[2,288,768]{2,1,0:T(8,128)(2,1)S(1)}, bf16[2,288,768]{2,1,0:T(8,128)(2,1)S(1)}, u32[]{:S(2)}, u32[]{:S(2)}) collective-permute-start(bf16[2,288,768]{2,1,0:T(8,128)(2,1)S(1)} %collective-permute-done.26.refs_5_), channel_id=1, source_target_pairs={{32,0},{48,16},{64,32},{80,48},{96,64},{112,80},{0,96},{16,112},{3... | collective-permute-start | bytes 2654216 | tf_op jit(solution)/shard_map/ppermute | solution.py:55
  166.7 21.9 %collective-permute-start.32 = (bf16[2,288,768]{2,1,0:T(8,128)(2,1)S(1)}, bf16[2,288,768]{2,1,0:T(8,128)(2,1)}, u32[]{:S(2)}, u32[]{:S(2)}) collective-permute-start(bf16[2,288,768]{2,1,0:T(8,128)(2,1)S(1)} %collective-permute-done.26.refs_5_), channel_id=1, source_target_pairs={{96,0},{112,16},{0,32},{16,48},{32,64},{48,80},{64,96},{80,112},{9... | collective-permute-start | bytes 2654216 | tf_op jit(solution)/shard_map/ppermute | solution.py:55
  188.6 32.1 %collective-permute-start.33 = (bf16[2,288,768]{2,1,0:T(8,128)(2,1)}, bf16[2,288,768]{2,1,0:T(8,128)(2,1)}, u32[]{:S(2)}, u32[]{:S(2)}) collective-permute-start(bf16[2,288,768]{2,1,0:T(8,128)(2,1)} %collective-permute-done.29.refs_6_), channel_id=1, source_target_pairs={{32,0},{48,16},{64,32},{80,48},{96,64},{112,80},{0,96},{16,112},{3... | collective-permute-start | bytes 2654216 | tf_op jit(solution)/shard_map/ppermute | solution.py:55
  189.0 31.6 %collective-permute-start.34 = (bf16[2,288,768]{2,1,0:T(8,128)(2,1)}, bf16[2,288,768]{2,1,0:T(8,128)(2,1)}, u32[]{:S(2)}, u32[]{:S(2)}) collective-permute-start(bf16[2,288,768]{2,1,0:T(8,128)(2,1)} %collective-permute-done.32.refs_11_), channel_id=1, source_target_pairs={{96,0},{112,16},{0,32},{16,48},{32,64},{48,80},{64,96},{80,112},{9... | collective-permute-start | bytes 2654216 | tf_op jit(solution)/shard_map/ppermute | solution.py:55
  193.4 22.6 %collective-permute-start.38 = (bf16[2,128,2048]{2,1,0:T(8,128)(2,1)}, bf16[2,128,2048]{2,1,0:T(8,128)(2,1)S(1)}, u32[]{:S(2)}, u32[]{:S(2)}) collective-permute-start(bf16[2,128,2048]{2,1,0:T(8,128)(2,1)} %get-tuple-element.83), channel_id=1, source_target_pairs={{6,0},{7,1},{0,2},{1,3},{2,4},{3,5},{4,6},{5,7},{14,8},{15,9},{8,1... | collective-permute-start | bytes 3145736 | tf_op jit(solution)/shard_map/ppermute | solution.py:51
  194.9 23.4 %collective-permute-start.39 = (bf16[2,128,2048]{2,1,0:T(8,128)(2,1)S(1)}, bf16[2,128,2048]{2,1,0:T(8,128)(2,1)}, u32[]{:S(2)}, u32[]{:S(2)}) collective-permute-start(bf16[2,128,2048]{2,1,0:T(8,128)(2,1)S(1)} %add_convert_fusion), channel_id=1, source_target_pairs={{2,0},{3,1},{4,2},{5,3},{6,4},{7,5},{0,6},{1,7},{10,8},{11,9},{12,... | collective-permute-start | bytes 3145736 | tf_op jit(solution)/shard_map/ppermute | solution.py:51
  (39 other events, 566.4 us)
